TPU v7x, 256 devices: a whole 4x4x8 slice. The times are simulated.
256 devices in a mesh: res: 128 (over x, z, y_lo, core), ch: 2 (over y_hi).
Axes of the slice: x: 4, y: 4 (y_hi: 2, y_lo: 2; y = y_hi * 2 + y_lo), z: 8, core: 2. Of those that a mesh axis runs over, the one named last changes fastest.
Arguments:
- pair: bfloat16 [512, 512, 128], P('res'), may hold values from -48 to 48
- norm_gain: float32 [128], replicated, may hold values from 0.4 to 1.6
- norm_bias: float32 [128], replicated, may hold values from -2.5 to 2.5
- left_weight: bfloat16 [128, 128], P(None, 'ch'), may hold values from -0.5 to 0.5
- left_gate: bfloat16 [128, 128], P(None, 'ch'), may hold values from -0.5 to 0.5
- right_weight: bfloat16 [128, 128], P(None, 'ch'), may hold values from -0.5 to 0.5
- right_gate: bfloat16 [128, 128], P(None, 'ch'), may hold values from -0.5 to 0.5
- tri_gain: float32 [128], P('ch'), may hold values from 0.4 to 1.6
- tri_bias: float32 [128], P('ch'), may hold values from -2.5 to 2.5
- out_weight: bfloat16 [128, 128], P('ch'), may hold values from -0.5 to 0.5
- out_gate: bfloat16 [128, 128], P(None, 'ch'), may hold values from -0.5 to 0.5
Outputs:
- updated: bfloat16 [512, 512, 128], P('res', None, 'ch')
All inputs are finite; a program needn't handle non-finite values.
Results may differ from a plain program's by a relative error of at most 0.0055.
Values may be sent and summed in bfloat16 or wider, within the bound.
No kernel may reach another device: no remote copies, remote signals or barrier semaphores. Data moves between devices by JAX's collectives and lax.ppermute only.
A program may use at most 192 MiB of HBM per device.

v0:
```python
import jax
import jax.numpy as jnp
from jax import lax
from jax.sharding import PartitionSpec as P


def layer_norm(values, gain, bias):
    values = values.astype(jnp.float32)
    row_mean = jnp.mean(values, -1, keepdims=True)
    centred = values - row_mean
    row_var = jnp.mean(centred * centred, -1, keepdims=True)
    return centred * lax.rsqrt(row_var + 1e-05) * gain + bias


def matmul(values, weight):
    flat = values.reshape(-1, values.shape[-1])
    result = jnp.dot(flat, weight, preferred_element_type=jnp.float32)
    return result.reshape(values.shape[:-1] + (weight.shape[1],))


def gated(normed, weight, gate):
    return (jax.nn.sigmoid(matmul(normed, gate)) * matmul(normed, weight)).astype(jnp.bfloat16)


def body(
    pair,
    norm_gain,
    norm_bias,
    left_weight,
    left_gate,
    right_weight,
    right_gate,
    tri_gain,
    tri_bias,
    out_weight,
    out_gate,
):
    normed = layer_norm(pair, norm_gain, norm_bias).astype(jnp.bfloat16)
    left_proj = gated(normed, left_weight, left_gate)
    right_proj = gated(normed, right_weight, right_gate)
    triangle = jnp.einsum(
        "ikc,jkc->ijc",
        left_proj,
        lax.all_gather(right_proj, "res", axis=0, tiled=True),
        preferred_element_type=jnp.float32,
    )
    channels = triangle.shape[-1] * lax.axis_size("ch")
    total_sum, total_square = lax.psum(
        (jnp.sum(triangle, -1), jnp.sum(triangle * triangle, -1)), "ch"
    )
    row_mean = (total_sum / channels)[..., None]
    row_var = (total_square / channels)[..., None] - row_mean * row_mean
    onormed = ((triangle - row_mean) * lax.rsqrt(row_var + 1e-05) * tri_gain + tri_bias).astype(
        jnp.bfloat16
    )
    projected = lax.psum_scatter(matmul(onormed, out_weight), "ch", scatter_dimension=2, tiled=True)
    gate_value = jax.nn.sigmoid(matmul(normed, out_gate))
    return (gate_value * projected).astype(jnp.bfloat16)


def solution(mesh):
    placed = (
        P("res", None, None),
        P(),
        P(),
        P(None, "ch"),
        P(None, "ch"),
        P(None, "ch"),
        P(None, "ch"),
        P("ch"),
        P("ch"),
        P("ch", None),
        P(None, "ch"),
    )
    return jax.shard_map(
        body, mesh=mesh, in_specs=placed, out_specs=P("res", None, "ch"), check_vma=False
    )
```

profile of v0, /device:TPU:6, one launch (start us, length us, event | category | flops | bytes accessed | tf_op | source)
XLA Modules:
  0.0 387.6 jit_solution(11086303155571068568)
XLA Ops:
  6.5 0.0 copy-start
  6.5 0.0 all-gather.2.cloned.1.call-start
  6.5 1.3 convert_reduce_fusion
  7.8 1.7 fusion.22
  9.5 1.8 fusion.33
  11.4 2.6 fusion.20
  14.0 0.0 all-gather.2.cloned.1.call-update
  14.0 0.0 reduce-scatter.2.cloned.1.call-start
  14.0 1.8 fusion.30
  15.9 0.0 copy-start.1
  15.9 0.0 copy-start.4
  15.9 0.0 copy-start.5
  15.9 0.0 copy-start.6
  15.9 1.9 fusion.19
  17.9 249.6 %all-gather.2.cloned.1.call-done = bf16[512,512,64]{1,2,0:T(8,128)(2,1)} async-done(((bf16[4,512,64]{1,2,0:T(8,128)(2,1)}), bf16[512,512,64]{1,2,0:T(8,128)(2,1)}) %all-gather.2.cloned.1.call-update) | async-done | bytes 33554448 | tf_op jit(solution)/shard_map/all_gather | solution.py:44
  267.4 73.0 %fusion.42 = (f32[4,512]{1,0:T(4,128)S(1)}, f32[4,512]{1,0:T(4,128)S(1)}, f32[4,512,64]{1,0,2:T(4,128)S(1)}) fusion(bf16[4,512,64]{1,2,0:T(8,128)(2,1)S(1)} %fusion.19, bf16[512,512,64]{1,2,0:T(8,128)(2,1)} %all-gather.2.cloned.1.call-done), kind=kOutput, calls=%fused_computation.46 | convolution fusion | flops 134606848 | bytes 34357248 | tf_op jit(solution)/shard_map/ikc,jkc->ijc/dot_general | solution.py:41
  340.4 11.1 %all-reduce = (f32[4,512]{1,0:T(4,128)S(1)}, f32[4,512]{1,0:T(4,128)S(1)}) all-reduce(f32[4,512]{1,0:T(4,128)S(1)} %get-tuple-element.6, f32[4,512]{1,0:T(4,128)S(1)} %get-tuple-element.5), channel_id=1, replica_groups=mesh['res'=128,'ch'=2] {'ch'}, use_global_device_ids=true, to_apply=%region_5.0 | all-reduce | flops 4096 | bytes 32768 | tf_op jit(solution)/shard_map/psum | solution.py:48
  351.6 0.0 copy-done.2
  351.6 0.0 copy-done.3
  351.6 0.2 add_convert_fusion
  351.8 1.3 fusion.26
  353.2 0.0 reduce-scatter.2.cloned.1.call-update
  353.2 24.9 %reduce-scatter.2.cloned.1.call-done = f32[4,512,64]{1,2,0:T(8,128)} async-done(((f32[4,512,128]{1,2,0:T(8,128)}), f32[4,512,64]{1,2,0:T(8,128)}) %reduce-scatter.2.cloned.1.call-update) | async-done | bytes 524304 | tf_op jit(solution)/shard_map/reduce_scatter | solution.py:56
  378.1 2.7 fusion.21
  (10 shorter events, 0.0 us)
Async XLA Ops:
  6.5 345.3 %copy-start = (bf16[64,128]{1,0:T(8,128)(2,1)S(1)}, bf16[64,128]{1,0:T(8,128)(2,1)}, u32[]{:S(2)}) copy-start(bf16[64,128]{1,0:T(8,128)(2,1)} %param.20) | copy-start | bytes 49156
  6.5 260.9 %all-gather.2.cloned.1.call-start = ((), (), s32[]{:S(2)}) async-start(), calls=%async_computation.1 | async-start | bytes 33816576 | tf_op jit(solution)/shard_map/all_gather | solution.py:44
  13.9 337.6 %copy-start.2 = (f32[64]{0:T(128)S(1)}, f32[64]{0:T(128)}, u32[]{:S(2)}) copy-start(f32[64]{0:T(128)} %param.19) | copy-start | bytes 772
  13.9 337.6 %copy-start.3 = (f32[64]{0:T(128)S(1)}, f32[64]{0:T(128)}, u32[]{:S(2)}) copy-start(f32[64]{0:T(128)} %param.18) | copy-start | bytes 772
  14.0 364.1 %reduce-scatter.2.cloned.1.call-start = ((), (), s32[]{:S(2)}) async-start(), calls=%async_computation.2 | async-start | bytes 1572864 | tf_op jit(solution)/shard_map/reduce_scatter | solution.py:56
  15.9 362.2 %copy-start.1 = (bf16[4,512,128]{2,1,0:T(8,128)(2,1)S(1)}, bf16[4,512,128]{2,1,0:T(8,128)(2,1)}, u32[]{:S(2)}) copy-start(bf16[4,512,128]{2,1,0:T(8,128)(2,1)} %param.11) | copy-start | bytes 1572868
  15.9 362.2 %copy-start.4 = (bf16[128,64]{0,1:T(8,128)(2,1)S(1)}, bf16[128,64]{0,1:T(8,128)(2,1)}, u32[]{:S(2)}) copy-start(bf16[128,64]{0,1:T(8,128)(2,1)} %param.21) | copy-start | bytes 49156
  15.9 362.2 %copy-start.5 = (f32[128]{0:T(128)S(1)}, f32[128]{0:T(128)}, u32[]{:S(2)}) copy-start(f32[128]{0:T(128)} %param.13) | copy-start | bytes 1540
  15.9 362.2 %copy-start.6 = (f32[128]{0:T(128)S(1)}, f32[128]{0:T(128)}, u32[]{:S(2)}) copy-start(f32[128]{0:T(128)} %param.12) | copy-start | bytes 1540
Sparse Core Ops, SparseCore 0:
  14.1 253.2 all-gather.1
  353.3 24.7 reduce-scatter.1
where the time goes:
time: 389 us; the launch traced here: 388 us
  waiting for transfers between devices  274 us (70%)
  matrix products  85.2 us (22%)
  between operations  13.5 us (3%)
  blocking collectives  11.1 us (3%)
    all_gather x1, waiting for transfers between devices, body(): lax.all_gather(right_proj, 'res', axis=0, tiled=True)  250 us
    dot_general x1, matrix products, body(): jnp.einsum('ikc,jkc->ijc', left_proj, lax.all_gather(right_proj, 'res', a...  73 us
    reduce_scatter x1, waiting for transfers between devices, body(): lax.psum_scatter(matmul(onormed, out_weight), 'ch', scatter_dimension=2,...  24.9 us
    dot_general x6, matrix products, matmul(): result = jnp.dot(flat, weight, preferred_element_type=jnp.float32)  12.2 us
    psum x1, blocking collectives, body(): lax.psum((jnp.sum(triangle, -1), jnp.sum(triangle * triangle, -1)), 'ch')  11.1 us
  transfers between devices with their start and end apart: 2, of which 2 were waited for; matrix products, arithmetic and copies ran while one was open for 1% of the time, Pallas kernels for 0%

commit v1 on v0

v1 whole, which is shorter than its diff:
```python
import jax
import jax.numpy as jnp
from jax import lax
from jax.sharding import Mesh, PartitionSpec as P

F32 = jnp.float32
BF16 = jnp.bfloat16
CHIPS = ("x", "z", "ylo")
RES = CHIPS + ("core",)


def layer_norm(values, gain, bias):
    values = values.astype(F32)
    row_mean = jnp.mean(values, -1, keepdims=True)
    centred = values - row_mean
    row_var = jnp.mean(centred * centred, -1, keepdims=True)
    return centred * lax.rsqrt(row_var + 1e-05) * gain + bias


def split2(values):
    high = values.astype(BF16)
    low = (values - high.astype(F32)).astype(BF16)
    return high, low


def body(
    pair,
    norm_gain,
    norm_bias,
    left_weight,
    left_gate,
    right_weight,
    right_gate,
    tri_gain,
    tri_bias,
    out_weight,
    out_gate,
):
    rows, tokens, channels = pair.shape
    own = left_weight.shape[1]
    me = lax.axis_index("yhi")
    swap = [(0, 1), (1, 0)]

    scaled = tri_gain[:, None] * out_weight.astype(F32)
    scaled_hi, scaled_lo = split2(scaled)
    gain_sum = jnp.sum(scaled, 0)
    bias_sum = jnp.sum(tri_bias[:, None] * out_weight.astype(F32), 0)
    sums = jnp.stack([gain_sum, bias_sum]).reshape(2, 2, own)
    sums_mine = lax.dynamic_index_in_dim(sums, me, 1, False)
    sums_other = lax.ppermute(lax.dynamic_index_in_dim(sums, 1 - me, 1, False), "yhi", swap)

    normed = layer_norm(pair, norm_gain, norm_bias).astype(BF16).reshape(-1, channels)
    weights = jnp.concatenate([left_gate, left_weight, right_gate, right_weight], 1)
    pre = lax.dot_general(weights, normed, (((0,), (1,)), ((), ())), preferred_element_type=F32)
    left = (jax.nn.sigmoid(pre[:own]) * pre[own : 2 * own]).astype(BF16)
    right = (jax.nn.sigmoid(pre[2 * own : 3 * own]) * pre[3 * own :]).astype(BF16)
    gate_value = jax.nn.sigmoid(
        lax.dot_general(out_gate, normed, (((0,), (1,)), ((), ())), preferred_element_type=F32)
    )

    sent = jnp.stack([left, right], 1).reshape(own, 2 * rows, tokens)
    got = lax.all_to_all(sent, CHIPS, 0, 0, tiled=True)
    left_all = got[:, :rows].reshape(-1, tokens)
    right_all = lax.all_gather(got[:, rows:], "core", axis=1, tiled=True).reshape(-1, tokens)
    triangle = lax.dot_general(
        left_all, right_all, (((1,), (1,)), ((), ())), preferred_element_type=F32
    ).astype(BF16)
    tri = lax.all_to_all(triangle.reshape(own, rows, tokens), CHIPS, 0, 0, tiled=True)
    tri = tri.reshape(own, -1)

    wide = tri.astype(F32)
    mean_mine = jnp.mean(wide, 0, keepdims=True)
    centred = wide - mean_mine
    square_mine = jnp.sum(centred * centred, 0, keepdims=True)
    part = lax.dot_general(
        jnp.concatenate([scaled_hi, scaled_lo], 0),
        jnp.concatenate([tri, tri], 0),
        (((0,), (0,)), ((), ())),
        preferred_element_type=F32,
    )
    part = part - gain_sum[:, None] * mean_mine
    part = part.reshape(2, own, -1)
    part_mine = lax.dynamic_index_in_dim(part, me, 0, False)
    part_other = lax.dynamic_index_in_dim(part, 1 - me, 0, False).astype(BF16)
    payload = jnp.concatenate([part_other, *split2(mean_mine), *split2(square_mine)], 0)
    payload = lax.ppermute(payload, "yhi", swap).astype(F32)

    mean_other = payload[own : own + 1] + payload[own + 1 : own + 2]
    square_other = payload[own + 2 : own + 3] + payload[own + 3 : own + 4]
    mean = 0.5 * (mean_mine + mean_other)
    half = 0.5 * (mean_mine - mean_other)
    var = (square_mine + square_other) / (2 * own) + half * half
    lean = (sums_mine[0] - sums_other[0])[:, None] * half
    projected = (part_mine + payload[:own] + lean) * lax.rsqrt(var + 1e-05)
    projected = projected + (sums_mine[1] + sums_other[1])[:, None]
    updated = (gate_value * projected).astype(BF16)
    return updated.T.reshape(rows, tokens, own)


def solution(mesh):
    fine = Mesh(mesh.devices.reshape(4, 8, 2, 2, 2), RES + ("yhi",))
    placed = (
        P(RES, None, None),
        P(),
        P(),
        P(None, "yhi"),
        P(None, "yhi"),
        P(None, "yhi"),
        P(None, "yhi"),
        P("yhi"),
        P("yhi"),
        P("yhi", None),
        P(None, "yhi"),
    )
    return jax.shard_map(
        body, mesh=fine, in_specs=placed, out_specs=P(RES, None, "yhi"), check_vma=False
    )
```

time: 389 us -> 69.9 us (0.18)
  waiting for transfers between devices: 274 us -> 16.7 us
  matrix products: 85.2 us -> 1.61 us
  blocking collectives: 11.1 us -> 31.7 us
  between operations: 13.5 us -> 0.3 us
  starting transfers between devices: 0.04 us -> 10.7 us
    all_gather x1 -> x0, waiting for transfers between devices: 250 us -> none  [body(): lax.all_gather(right_proj, 'res', axis=0, tiled=True)]
    dot_general x7 -> x4, matrix products: 85.2 us -> 1.61 us  [the longest x1 0.49 us: body(): lax.dot_general(left_all, right_all, (((1,), (1,)), ((), ())), preferred_...]
    all_to_all x0 -> x1, blocking collectives: none -> 29.5 us  [body(): got = lax.all_to_all(sent, CHIPS, 0, 0, tiled=True)]
    reduce_scatter x1 -> x0, waiting for transfers between devices: 24.9 us -> none  [body(): lax.psum_scatter(matmul(onormed, out_weight), 'ch', scatter_dimension=2,...]
    all_to_all x0 -> x1, waiting for transfers between devices: none -> 11.4 us  [body(): lax.all_to_all(triangle.reshape(own, rows, tokens), CHIPS, 0, 0, tiled=True)]
    psum x1 -> x0, blocking collectives: 11.1 us -> none  [body(): lax.psum((jnp.sum(triangle, -1), jnp.sum(triangle * triangle, -1)), 'ch')]
    all_to_all x0 -> x1, starting transfers between devices: none -> 7.1 us  [body(): lax.all_to_all(triangle.reshape(own, rows, tokens), CHIPS, 0, 0, tiled=True)]
    ppermute x0 -> x2, waiting for transfers between devices: none -> 5.35 us  [the longest x1 5.35 us: body(): lax.ppermute(lax.dynamic_index_in_dim(sums, 1 - me, 1, False), 'yhi', swap)]
  transfers between devices with their start and end apart: 2 -> 3, of which waited for: 2 -> 2; matrix products, arithmetic and copies ran while one was open for 1% -> 0% of each run, Pallas kernels for 0% -> 0%
where the time goes in v1:
time: 69.9 us; the launch traced here: 69.6 us
  blocking collectives  31.7 us (45%)
  waiting for transfers between devices  16.7 us (24%)
  starting transfers between devices  10.7 us (15%)
  other arithmetic  5.57 us (8%)
  local copies, waits for them, and re-layouts  2.92 us (4%)
  matrix products  1.61 us (2%)
    all_to_all x1, blocking collectives, body(): got = lax.all_to_all(sent, CHIPS, 0, 0, tiled=True)  29.5 us
    all_to_all x1, waiting for transfers between devices, body(): lax.all_to_all(triangle.reshape(own, rows, tokens), CHIPS, 0, 0, tiled=True)  11.4 us
    all_to_all x1, starting transfers between devices, body(): lax.all_to_all(triangle.reshape(own, rows, tokens), CHIPS, 0, 0, tiled=True)  7.1 us
    ppermute x1, waiting for transfers between devices, body(): lax.ppermute(lax.dynamic_index_in_dim(sums, 1 - me, 1, False), 'yhi', swap)  5.35 us
    ppermute x1, starting transfers between devices, body(): payload = lax.ppermute(payload, 'yhi', swap).astype(F32)  2.99 us
    all_gather x1, blocking collectives, body(): lax.all_gather(got[:, rows:], 'core', axis=1, tiled=True)  2.18 us
    reduce_sum x1, other arithmetic, layer_norm(): row_var = jnp.mean(centred * centred, -1, keepdims=True)  1.68 us
    convert_element_type x1, other arithmetic, body(): layer_norm(pair, norm_gain, norm_bias).astype(BF16).reshape(-1, channels)  1.67 us
  transfers between devices with their start and end apart: 3, of which 2 were waited for; matrix products, arithmetic and copies ran while one was open for 0% of the time, Pallas kernels for 0%

profile of v1, /device:TPU:6, one launch (start us, length us, event | category | flops | bytes accessed | tf_op | source)
XLA Modules:
  0.0 69.6 jit_solution(13902669424833186085)
XLA Ops:
  0.0 1.3 %convert_reduce_fusion = f32[4,512]{1,0:T(4,128)S(1)} fusion(bf16[4,512,128]{2,1,0:T(8,128)(2,1)} %param.11), kind=kLoop, calls=%fused_computation.7 | loop fusion | flops 522240 | bytes 532480 | tf_op jit(solution)/shard_map/reduce_sum | solution.py:14
  1.3 1.7 %fusion.6 = f32[4,512]{1,0:T(4,128)S(1)} fusion(bf16[4,512,128]{2,1,0:T(8,128)(2,1)} %param.11, f32[4,512]{1,0:T(4,128)S(1)} %broadcast_multiply_fusion.1), kind=kLoop, calls=%fused_computation.11 | loop fusion | flops 1046528 | bytes 540672 | tf_op jit(solution)/shard_map/reduce_sum | solution.py:16
  3.0 1.7 %fusion.9 = bf16[4,512,128]{2,1,0:T(8,128)(2,1)S(1)} fusion(bf16[4,512,128]{2,1,0:T(8,128)(2,1)} %param.11, f32[128]{0:T(128)} %param.13, f32[128]{0:T(128)} %param.12, f32[4,512]{1,0:T(4,128)S(1)} %add_rsqrt_fusion.1, f32[4,512]{1,0:T(4,128)S(1)} %broadcast_multiply_fusion.1), kind=kLoop, calls=%fused_computation.14 | loop fusion | flops 1572864 | bytes 1065984 | tf_op jit(solution)/shard_map/convert_element_type | solution.py:52
  4.8 0.4 fusion.33
  5.2 0.3 fusion.31
  5.5 0.5 copy.18
  6.1 0.1 reshape.156
  6.2 29.5 %all_to_all.10 = bf16[64,8,512]{2,1,0:T(8,128)(2,1)S(1)} all-to-all(bf16[64,8,512]{2,1,0:T(8,128)(2,1)S(1)} %reshape.156), channel_id=1, replica_groups=mesh['x'=4,'z'=8,'ylo'=2,'core'=2,'yhi'=2] {'x','z','ylo'}, dimensions={0} | all-to-all | bytes 1048576 | tf_op jit(solution)/shard_map/all_to_all | solution.py:62
  35.7 0.2 fusion.61
  36.0 2.2 %all_gather.3 = bf16[64,8,512]{2,0,1:T(8,128)(2,1)S(1)} all-gather(bf16[64,4,512]{2,0,1:T(8,128)(2,1)S(1)} %copy.19), channel_id=1, replica_groups=mesh['x'=4,'z'=8,'ylo'=2,'core'=2,'yhi'=2] {'core'}, dimensions={1}, use_global_device_ids=true | all-gather | bytes 786432 | tf_op jit(solution)/shard_map/all_gather | solution.py:64
  38.3 0.5 convolution_convert_fusion
  38.8 0.8 %reshape.159 = bf16[64,4,512]{2,1,0:T(4,128)(2,1)} reshape(bf16[256,512]{1,0:T(8,128)(2,1)S(1)} %convolution_convert_fusion) | data formatting | bytes 524288 | tf_op jit(solution)/shard_map/reshape | solution.py:68
  39.5 7.1 %all-to-all-start.1 = ((bf16[64,4,512]{2,1,0:T(4,128)(2,1)}), bf16[64,4,512]{2,1,0:T(4,128)(2,1)S(1)}, u32[]{:S(2)}, u32[]{:S(2)}) async-start(bf16[64,4,512]{2,1,0:T(4,128)(2,1)} %reshape.159), calls=%async_computation.1 | async-start | bytes 524288 | tf_op jit(solution)/shard_map/all_to_all | solution.py:68
  46.7 0.1 fusion.43
  47.0 11.4 %all-to-all-done.1 = bf16[64,4,512]{2,1,0:T(4,128)(2,1)S(1)} async-done(((bf16[64,4,512]{2,1,0:T(4,128)(2,1)}), bf16[64,4,512]{2,1,0:T(4,128)(2,1)S(1)}, u32[]{:S(2)}, u32[]{:S(2)}) %all-to-all-start.1) | async-done | bytes 262176 | tf_op jit(solution)/shard_map/all_to_all | solution.py:68
  58.3 0.1 convert_reduce_fusion.1
  58.5 0.2 fusion.11
  58.8 0.3 convolution_subtract_fusion
  59.2 0.2 concatenate.16
  59.3 3.0 %collective-permute-start = (bf16[68,2048]{1,0:T(8,128)(2,1)S(1)}, bf16[68,2048]{1,0:T(8,128)(2,1)S(1)}, u32[]{:S(2)}, u32[]{:S(2)}) collective-permute-start(bf16[68,2048]{1,0:T(8,128)(2,1)S(1)} %concatenate.16), channel_id=1, source_target_pairs={{0,1},{1,0},{2,3},{3,2},{4,5},{5,4},{6,7},{7,6},{8,9},{9,8},{10,11... | collective-permute-start | bytes 835592 | tf_op jit(solution)/shard_map/ppermute | solution.py:86
  62.3 0.6 collective-permute-start.1
  63.0 5.4 %collective-permute-done.1 = f32[2,64]{1,0:T(2,128)S(1)} collective-permute-done((f32[2,64]{1,0:T(2,128)S(1)}, f32[2,64]{1,0:T(2,128)S(1)}, u32[]{:S(2)}, u32[]{:S(2)}) %collective-permute-start.1) | collective-permute-done | bytes 544 | tf_op jit(solution)/shard_map/ppermute | solution.py:50
  68.5 0.4 fusion.16
  68.8 0.7 %copy.32 = bf16[8,4,8,512]{3,2,0,1:T(8,128)(2,1)} copy(bf16[8,4,8,512]{3,2,1,0:T(8,128)(2,1)S(1)} %bitcast.59) | data formatting | bytes 524288 | tf_op jit(solution)/shard_map/reshape | solution.py:97
  (39 shorter events, 0.6 us)
Async XLA Ops:
  0.0 68.4 %copy-start = (bf16[128,64]{0,1:T(8,128)(2,1)S(1)}, bf16[128,64]{0,1:T(8,128)(2,1)}, u32[]{:S(2)}) copy-start(bf16[128,64]{0,1:T(8,128)(2,1)} %param.21) | copy-start | bytes 49156
  0.0 4.7 %copy-start.3 = (bf16[128,64]{0,1:T(8,128)(2,1)S(1)}, bf16[128,64]{0,1:T(8,128)(2,1)}, u32[]{:S(2)}) copy-start(bf16[128,64]{0,1:T(8,128)(2,1)} %param.14) | copy-start | bytes 49156
  0.0 4.7 %copy-start.4 = (bf16[128,64]{0,1:T(8,128)(2,1)S(1)}, bf16[128,64]{0,1:T(8,128)(2,1)}, u32[]{:S(2)}) copy-start(bf16[128,64]{0,1:T(8,128)(2,1)} %param.15) | copy-start | bytes 49156
  0.0 4.7 %copy-start.1 = (bf16[128,64]{0,1:T(8,128)(2,1)S(1)}, bf16[128,64]{0,1:T(8,128)(2,1)}, u32[]{:S(2)}) copy-start(bf16[128,64]{0,1:T(8,128)(2,1)} %param.16) | copy-start | bytes 49156
  0.0 4.7 %copy-start.2 = (bf16[128,64]{0,1:T(8,128)(2,1)S(1)}, bf16[128,64]{0,1:T(8,128)(2,1)}, u32[]{:S(2)}) copy-start(bf16[128,64]{0,1:T(8,128)(2,1)} %param.17) | copy-start | bytes 49156
  35.9 10.7 %copy-start.5 = (bf16[64,128]{1,0:T(8,128)(2,1)S(1)}, bf16[64,128]{1,0:T(8,128)(2,1)}, u32[]{:S(2)}) copy-start(bf16[64,128]{1,0:T(8,128)(2,1)} %param.20) | copy-start | bytes 49156
  35.9 10.7 %copy-start.6 = (f32[64]{0:T(128)S(1)}, f32[64]{0:T(128)}, u32[]{:S(2)}) copy-start(f32[64]{0:T(128)} %param.18) | copy-start | bytes 772
  35.9 10.7 %copy-start.7 = (f32[64]{0:T(128)S(1)}, f32[64]{0:T(128)}, u32[]{:S(2)}) copy-start(f32[64]{0:T(128)} %param.19) | copy-start | bytes 772
  39.5 18.8 %all-to-all-start.1 = ((bf16[64,4,512]{2,1,0:T(4,128)(2,1)}), bf16[64,4,512]{2,1,0:T(4,128)(2,1)S(1)}, u32[]{:S(2)}, u32[]{:S(2)}) async-start(bf16[64,4,512]{2,1,0:T(4,128)(2,1)} %reshape.159), calls=%async_computation.1 | async-start | bytes 524288 | tf_op jit(solution)/shard_map/all_to_all | solution.py:68
  59.3 9.0 %collective-permute-start = (bf16[68,2048]{1,0:T(8,128)(2,1)S(1)}, bf16[68,2048]{1,0:T(8,128)(2,1)S(1)}, u32[]{:S(2)}, u32[]{:S(2)}) collective-permute-start(bf16[68,2048]{1,0:T(8,128)(2,1)S(1)} %concatenate.16), channel_id=1, source_target_pairs={{0,1},{1,0},{2,3},{3,2},{4,5},{5,4},{6,7},{7,6},{8,9},{9,8},{10,11... | collective-permute-start | bytes 835592 | tf_op jit(solution)/shard_map/ppermute | solution.py:86
  62.3 6.0 %collective-permute-start.1 = (f32[2,64]{1,0:T(2,128)S(1)}, f32[2,64]{1,0:T(2,128)S(1)}, u32[]{:S(2)}, u32[]{:S(2)}) collective-permute-start(f32[2,64]{1,0:T(2,128)S(1)} %bitcast.70), channel_id=1, source_target_pairs={{0,1},{1,0},{2,3},{3,2},{4,5},{5,4},{6,7},{7,6},{8,9},{9,8},{10,11... | collective-permute-start | bytes 1544 | tf_op jit(solution)/shard_map/ppermute | solution.py:50

commit v2 on v1

v2 whole, which is shorter than its diff:
```python
import jax
import jax.numpy as jnp
from jax import lax
from jax.experimental import pallas as pl
from jax.experimental.pallas import tpu as pltpu
from jax.sharding import Mesh, PartitionSpec as P

F32 = jnp.float32
BF16 = jnp.bfloat16
CHIPS = ("x", "z", "ylo")
RES = CHIPS + ("core",)
EPS = 1e-05


def project_kernel(pair_ref, gain_ref, bias_ref, weight_ref, sent_ref, gate_ref):
    own = gate_ref.shape[1]
    values = pair_ref[0].astype(F32)
    centred = values - jnp.mean(values, -1, keepdims=True)
    row_var = jnp.mean(centred * centred, -1, keepdims=True)
    normed = (centred * lax.rsqrt(row_var + EPS) * gain_ref[...] + bias_ref[...]).astype(BF16)
    pre = lax.dot_general(
        weight_ref[...], normed, (((1,), (1,)), ((), ())), preferred_element_type=F32
    )
    left = jax.nn.sigmoid(pre[:own]) * pre[own : 2 * own]
    right = jax.nn.sigmoid(pre[2 * own : 3 * own]) * pre[3 * own : 4 * own]
    sent_ref[0, 0] = left.astype(BF16)
    sent_ref[1, 0] = right.astype(BF16)
    gate_ref[0] = jax.nn.sigmoid(pre[4 * own :])


def finish_kernel(tri_ref, gate_ref, weight_ref, gain_ref, bias_ref, out_ref):
    values = tri_ref[0].astype(F32)
    centred = values - jnp.mean(values, 0, keepdims=True)
    var = jnp.mean(centred * centred, 0, keepdims=True)
    onormed = (centred * lax.rsqrt(var + EPS) * gain_ref[...] + bias_ref[...]).astype(BF16)
    projected = jnp.dot(weight_ref[...], onormed, preferred_element_type=F32)
    out_ref[0] = (gate_ref[0] * projected).astype(BF16)


def whole(shape):
    return pl.BlockSpec(shape, lambda i: (0,) * len(shape))


def body(
    pair,
    norm_gain,
    norm_bias,
    left_weight,
    left_gate,
    right_weight,
    right_gate,
    tri_gain,
    tri_bias,
    out_weight,
    out_gate,
):
    rows, tokens, channels = pair.shape
    own = left_weight.shape[1]
    me = lax.axis_index("yhi")
    swap = [(0, 1), (1, 0)]

    columns = out_weight.T.reshape(2, own, own)
    extra = jnp.stack([tri_gain, tri_bias])
    mine = lax.dynamic_index_in_dim(columns, me, 0, False).astype(F32)
    theirs = lax.dynamic_index_in_dim(columns, 1 - me, 0, False).astype(F32)
    mine = jnp.concatenate([mine, extra], 0)
    other = lax.ppermute(jnp.concatenate([theirs, extra], 0), "yhi", swap)
    table = jnp.where(
        me == 0, jnp.concatenate([mine, other], 1), jnp.concatenate([other, mine], 1)
    )

    weights = jnp.concatenate(
        [left_gate.T, left_weight.T, right_gate.T, right_weight.T, out_gate.T], 0
    )
    sent, gate_value = pl.pallas_call(
        project_kernel,
        grid=(rows,),
        in_specs=[
            pl.BlockSpec((1, tokens, channels), lambda i: (i, 0, 0)),
            whole((1, channels)),
            whole((1, channels)),
            whole(weights.shape),
        ],
        out_specs=[
            pl.BlockSpec((2, 1, own, tokens), lambda i: (0, i, 0, 0)),
            pl.BlockSpec((1, own, tokens), lambda i: (i, 0, 0)),
        ],
        out_shape=[
            jax.ShapeDtypeStruct((2, rows, own, tokens), BF16),
            jax.ShapeDtypeStruct((rows, own, tokens), F32),
        ],
        name="project",
    )(pair, norm_gain[None], norm_bias[None], weights)

    sent = sent.reshape(2 * rows, own, tokens).swapaxes(0, 1)
    got = lax.all_to_all(sent, CHIPS, 0, 0, tiled=True)
    left_all = got[:, :rows].reshape(-1, tokens)
    right_all = lax.all_gather(got[:, rows:], "core", axis=1, tiled=True).reshape(-1, tokens)
    triangle = lax.dot_general(
        left_all, right_all, (((1,), (1,)), ((), ())), preferred_element_type=F32
    ).astype(BF16)
    triangle = jnp.broadcast_to(triangle.reshape(1, own, rows, tokens), (2, own, rows, tokens))
    tri = lax.all_to_all(
        triangle.reshape(2 * own, rows, tokens), ("yhi",) + CHIPS, 0, 0, tiled=True
    ).swapaxes(0, 1)

    updated = pl.pallas_call(
        finish_kernel,
        grid=(rows,),
        in_specs=[
            pl.BlockSpec((1, channels, tokens), lambda i: (i, 0, 0)),
            pl.BlockSpec((1, own, tokens), lambda i: (i, 0, 0)),
            whole((own, channels)),
            whole((channels, 1)),
            whole((channels, 1)),
        ],
        out_specs=pl.BlockSpec((1, own, tokens), lambda i: (i, 0, 0)),
        out_shape=jax.ShapeDtypeStruct((rows, own, tokens), BF16),
        name="finish",
    )(
        tri,
        gate_value,
        table[:own].astype(BF16),
        table[own].reshape(-1, 1),
        table[own + 1].reshape(-1, 1),
    )
    return updated.swapaxes(1, 2)


def solution(mesh):
    fine = Mesh(mesh.devices.reshape(4, 8, 2, 2, 2), RES + ("yhi",))
    placed = (
        P(RES, None, None),
        P(),
        P(),
        P(None, "yhi"),
        P(None, "yhi"),
        P(None, "yhi"),
        P(None, "yhi"),
        P("yhi"),
        P("yhi"),
        P("yhi", None),
        P(None, "yhi"),
    )
    return jax.shard_map(
        body, mesh=fine, in_specs=placed, out_specs=P(RES, None, "yhi"), check_vma=False
    )
```

time: 69.9 us -> 76.9 us (1.10); the launches traced: 69.6 us -> 75.4 us
  Pallas kernels: 0 us -> 8.02 us
  local copies, waits for them, and re-layouts: 2.92 us -> 9.9 us
  other arithmetic: 5.57 us -> 0.11 us
  waiting for transfers between devices: 16.7 us -> 11.5 us
  starting transfers between devices: 10.7 us -> 13.6 us
  matrix products: 1.61 us -> 0.49 us
    pallas_call x0 -> x2, Pallas kernels: none -> 8.02 us  [the longest x1 4.23 us: body(): pl.pallas_call(project_kernel, grid=(rows,), in_specs=[pl.BlockSpec((1, t...]
    unnamed x21 -> x20, local copies, waits for them, and re-layouts: 0.11 us -> 4.18 us
    reduce_sum x4 -> x0, other arithmetic: 3.32 us -> none  [the longest x1 1.68 us: layer_norm(): row_var = jnp.mean(centred * centred, -1, keepdims=True)]
    ppermute x2 -> x1, waiting for transfers between devices: 5.35 us -> 2.18 us  [body(): other = lax.ppermute(jnp.concatenate([theirs, extra], 0), 'yhi', swap)]
    all_to_all x1, starting transfers between devices: 7.1 us -> 10.1 us  [body(): lax.all_to_all(triangle.reshape(2 * own, rows, tokens), ('yhi',) + CHIPS,...]
    all_to_all x1, waiting for transfers between devices: 11.4 us -> 9.28 us  [body(): lax.all_to_all(triangle.reshape(2 * own, rows, tokens), ('yhi',) + CHIPS,...]
    convert_element_type x6 -> x1, other arithmetic: 1.84 us -> 0.01 us  [body(): mine = lax.dynamic_index_in_dim(columns, me, 0, False).astype(F32)]
    dot_general x3 -> x0, matrix products: 1.12 us -> none  [the longest x1 0.44 us: body(): lax.dot_general(weights, normed, (((0,), (1,)), ((), ())), preferred_elem...]
  transfers between devices with their start and end apart: 3 -> 2, of which waited for: 2 -> 2; matrix products, arithmetic and copies ran while one was open for 0% -> 3% of each run, Pallas kernels for 0% -> 0%
where the time goes in v2:
time: 76.9 us; the launch traced here: 75.4 us
  blocking collectives  31.7 us (41%)
  starting transfers between devices  13.6 us (18%)
  waiting for transfers between devices  11.5 us (15%)
  local copies, waits for them, and re-layouts  9.9 us (13%)
  Pallas kernels  8.02 us (10%)
    all_to_all x1, blocking collectives, body(): got = lax.all_to_all(sent, CHIPS, 0, 0, tiled=True)  29.5 us
    all_to_all x1, starting transfers between devices, body(): lax.all_to_all(triangle.reshape(2 * own, rows, tokens), ('yhi',) + CHIPS,...  10.1 us
    all_to_all x1, waiting for transfers between devices, body(): lax.all_to_all(triangle.reshape(2 * own, rows, tokens), ('yhi',) + CHIPS,...  9.28 us
    pallas_call x1, Pallas kernels, body(): pl.pallas_call(project_kernel, grid=(rows,), in_specs=[pl.BlockSpec((1, t...  4.23 us
    unnamed x20, local copies, waits for them, and re-layouts  4.18 us
    pallas_call x1, Pallas kernels, body(): pl.pallas_call(finish_kernel, grid=(rows,), in_specs=[pl.BlockSpec((1, ch...  3.79 us
    ppermute x1, starting transfers between devices, body(): other = lax.ppermute(jnp.concatenate([theirs, extra], 0), 'yhi', swap)  3.49 us
    all_gather x1, blocking collectives, body(): lax.all_gather(got[:, rows:], 'core', axis=1, tiled=True)  2.18 us
  transfers between devices with their start and end apart: 2, of which 2 were waited for; matrix products, arithmetic and copies ran while one was open for 3% of the time, Pallas kernels for 0%

profile of v2, /device:TPU:6, one launch (start us, length us, event | category | flops | bytes accessed | tf_op | source)
XLA Modules:
  0.0 75.4 jit_solution(10199848223162196800)
XLA Ops:
  0.0 0.7 bitcast_dynamic-update-slice_fusion.4
  0.7 0.7 copy-done.3
  1.5 0.7 copy-done.4
  2.2 0.7 copy-done.5
  2.9 0.6 copy-done
  3.5 4.2 %project.1 = (bf16[2,4,64,512]{3,2,1,0:T(8,128)(2,1)}, f32[4,64,512]{2,1,0:T(8,128)}) custom-call(bf16[4,512,128]{2,1,0:T(8,128)(2,1)} %pair_ref.1, f32[1,128]{1,0:T(1,128)} %bitcast.48, f32[1,128]{1,0:T(1,128)} %bitcast.49, bf16[320,128]{1,0:T(8,128)(2,1)} %copy-done), custom_call_target="tpu_custom_call" | custom-call | tf_op jit(solution)/shard_map/project/pallas_call | solution.py:75
  7.8 1.3 %copy.41 = bf16[8,64,512]{2,0,1:T(8,128)(2,1)S(1)} copy(bf16[8,64,512]{2,1,0:T(8,128)(2,1)} %bitcast.41) | data formatting | bytes 1048576 | tf_op jit(solution)/shard_map/reshape | solution.py:95
  9.1 29.5 %all_to_all.10 = bf16[64,8,512]{2,1,0:T(8,128)(2,1)S(1)} all-to-all(bf16[64,8,512]{2,1,0:T(8,128)(2,1)S(1)} %bitcast.39), channel_id=1, replica_groups=mesh['x'=4,'z'=8,'ylo'=2,'core'=2,'yhi'=2] {'x','z','ylo'}, dimensions={0} | all-to-all | bytes 1048576 | tf_op jit(solution)/shard_map/all_to_all | solution.py:96
  38.6 0.2 fusion.2
  38.9 2.2 %all_gather.3 = bf16[64,8,512]{2,0,1:T(8,128)(2,1)S(1)} all-gather(bf16[64,4,512]{2,0,1:T(8,128)(2,1)S(1)} %copy.28), channel_id=1, replica_groups=mesh['x'=4,'z'=8,'ylo'=2,'core'=2,'yhi'=2] {'core'}, dimensions={1}, use_global_device_ids=true | all-gather | bytes 786432 | tf_op jit(solution)/shard_map/all_gather | solution.py:98
  41.1 0.5 convolution_convert_fusion
  41.7 0.9 %broadcast_in_dim.16 = bf16[2,64,4,512]{3,2,1,0:T(4,128)(2,1)} broadcast(bf16[64,4,512]{2,1,0:T(4,128)(2,1)S(1)} %broadcast_in_dim.15), dimensions={1,2,3} | broadcast | bytes 786432 | tf_op jit(solution)/shard_map/broadcast_in_dim | solution.py:102
  42.6 10.1 %all-to-all-start.1 = ((bf16[128,4,512]{2,1,0:T(4,128)(2,1)}), bf16[128,4,512]{2,1,0:T(4,128)(2,1)S(1)}, u32[]{:S(2)}, u32[]{:S(2)}) async-start(bf16[128,4,512]{2,1,0:T(4,128)(2,1)} %bitcast.10), calls=%async_computation.1 | async-start | bytes 1048576 | tf_op jit(solution)/shard_map/all_to_all | solution.py:103
  52.7 0.1 copy.31
  52.9 0.6 copy-done.6
  53.6 3.5 %collective-permute-start = (f32[66,64]{1,0:T(8,128)S(1)}, f32[66,64]{1,0:T(8,128)S(1)}, u32[]{:S(2)}, u32[]{:S(2)}) collective-permute-start(f32[66,64]{1,0:T(8,128)S(1)} %pad_maximum_fusion), channel_id=1, source_target_pairs={{0,1},{1,0},{2,3},{3,2},{4,5},{5,4},{6,7},{7,6},{8,9},{9,8},{10,11... | collective-permute-start | bytes 50696 | tf_op jit(solution)/shard_map/ppermute | solution.py:67
  57.1 2.2 %collective-permute-done = f32[66,64]{1,0:T(8,128)S(1)} collective-permute-done((f32[66,64]{1,0:T(8,128)S(1)}, f32[66,64]{1,0:T(8,128)S(1)}, u32[]{:S(2)}, u32[]{:S(2)}) %collective-permute-start) | collective-permute-done | bytes 16928 | tf_op jit(solution)/shard_map/ppermute | solution.py:67
  59.2 0.1 maximum_select_fusion
  59.3 0.6 slice.29.weight_ref
  59.9 0.7 copy.32.gain_ref
  60.7 0.7 copy.33.bias_ref
  61.4 9.3 %all-to-all-done.1 = bf16[128,4,512]{2,1,0:T(4,128)(2,1)S(1)} async-done(((bf16[128,4,512]{2,1,0:T(4,128)(2,1)}), bf16[128,4,512]{2,1,0:T(4,128)(2,1)S(1)}, u32[]{:S(2)}, u32[]{:S(2)}) %all-to-all-start.1) | async-done | bytes 524320 | tf_op jit(solution)/shard_map/all_to_all | solution.py:103
  70.7 0.9 %copy.40 = bf16[128,4,512]{2,0,1:T(8,128)(2,1)} copy(bf16[128,4,512]{2,1,0:T(4,128)(2,1)S(1)} %all-to-all-done.1) | data formatting | bytes 1048576 | tf_op jit(solution)/shard_map/all_to_all | solution.py:103
  71.6 3.8 %finish.1 = bf16[4,64,512]{2,1,0:T(8,128)(2,1)} custom-call(bf16[4,128,512]{2,1,0:T(8,128)(2,1)} %bitcast.40, f32[4,64,512]{2,1,0:T(8,128)} %get-tuple-element.8.gate_ref, bf16[64,128]{1,0:T(8,128)(2,1)} %slice.29.weight_ref, f32[128,1]{1,0:T(8,128)} %copy.32.gain_ref, f32[128,1]{1,0:T(8,128)} %copy.33.bias_ref), custom_call_target="tpu_custom_call" | custom-call | tf_op jit(solution)/shard_map/finish/pallas_call | solution.py:107
  (21 shorter events, 0.3 us)
Async XLA Ops:
  0.0 0.7 copy-start.2
  0.7 0.7 copy-start.3
  1.5 0.7 copy-start.4
  2.2 0.7 copy-start.5
  2.9 0.6 copy-start
  42.6 10.1 %copy-start.1 = (bf16[64,128]{1,0:T(8,128)(2,1)S(1)}, bf16[64,128]{1,0:T(8,128)(2,1)}, u32[]{:S(2)}) copy-start(bf16[64,128]{1,0:T(8,128)(2,1)} %param.20) | copy-start | bytes 49156
  42.6 28.1 %all-to-all-start.1 = ((bf16[128,4,512]{2,1,0:T(4,128)(2,1)}), bf16[128,4,512]{2,1,0:T(4,128)(2,1)S(1)}, u32[]{:S(2)}, u32[]{:S(2)}) async-start(bf16[128,4,512]{2,1,0:T(4,128)(2,1)} %bitcast.10), calls=%async_computation.1 | async-start | bytes 1048576 | tf_op jit(solution)/shard_map/all_to_all | solution.py:103
  52.9 0.7 copy-start.6
  52.9 0.7 copy-start.7
  53.6 5.7 %collective-permute-start = (f32[66,64]{1,0:T(8,128)S(1)}, f32[66,64]{1,0:T(8,128)S(1)}, u32[]{:S(2)}, u32[]{:S(2)}) collective-permute-start(f32[66,64]{1,0:T(8,128)S(1)} %pad_maximum_fusion), channel_id=1, source_target_pairs={{0,1},{1,0},{2,3},{3,2},{4,5},{5,4},{6,7},{7,6},{8,9},{9,8},{10,11... | collective-permute-start | bytes 50696 | tf_op jit(solution)/shard_map/ppermute | solution.py:67

commit v3 on v1

v3 whole, which is shorter than its diff:
```python
import jax
import jax.numpy as jnp
from jax import lax
from jax.sharding import Mesh, PartitionSpec as P

F32 = jnp.float32
BF16 = jnp.bfloat16
CHIPS = ("x", "z", "ylo")
RES = CHIPS + ("core",)
EPS = 1e-05
SWAP = [(0, 1), (1, 0)]


def normalise(values, axis, gain, bias):
    centred = values - jnp.mean(values, axis, keepdims=True)
    var = jnp.mean(centred * centred, axis, keepdims=True)
    return (centred * lax.rsqrt(var + EPS) * gain[:, None] + bias[:, None]).astype(BF16)


def split3(values):
    high = values.astype(BF16)
    rest = values - high.astype(F32)
    middle = rest.astype(BF16)
    return jnp.stack([high, middle, (rest - middle.astype(F32)).astype(BF16)])


def per_row(matrix, values):
    matrix = jnp.broadcast_to(matrix, values.shape[:1] + matrix.shape)
    return lax.dot_general(matrix, values, (((2,), (1,)), ((0,), (0,))), preferred_element_type=F32)


def body(
    pair,
    norm_gain,
    norm_bias,
    left_weight,
    left_gate,
    right_weight,
    right_gate,
    tri_gain,
    tri_bias,
    out_weight,
    out_gate,
):
    rows, tokens, channels = pair.shape
    own = left_weight.shape[1]

    eye = jnp.broadcast_to(jnp.eye(channels, dtype=BF16), (rows, channels, channels))
    wide = lax.dot_general(eye, pair, (((2,), (2,)), ((0,), (0,))), preferred_element_type=F32)
    normed = normalise(wide, 1, norm_gain, norm_bias)
    weights = [left_gate.T, left_weight.T, right_gate.T, right_weight.T]
    pre = per_row(jnp.concatenate(weights, 0), normed)
    left = (jax.nn.sigmoid(pre[:, :own]) * pre[:, own : 2 * own]).astype(BF16)
    right = (jax.nn.sigmoid(pre[:, 2 * own : 3 * own]) * pre[:, 3 * own :]).astype(BF16)
    sent = jnp.concatenate([left, right], 0).transpose(1, 0, 2)
    first = lax.axis_index("core") == 0
    half = lax.axis_index("yhi") * own
    sent, first, half = lax.optimization_barrier((sent, first, half))

    got = lax.all_to_all(sent, CHIPS, 0, 0, tiled=True)
    got, out_weight, tri_gain, tri_bias = lax.optimization_barrier(
        (got, out_weight, tri_gain, tri_bias)
    )
    right_own = got[:, rows:]
    right_other = lax.ppermute(right_own, "core", SWAP)
    extra = split3(jnp.stack([tri_gain, tri_bias]))
    extra = jnp.concatenate([out_weight.reshape(-1), extra.reshape(-1)])
    extra = jnp.pad(extra, (0, -extra.size % (rows * tokens))).reshape(-1, rows, tokens)
    right_other, extra = lax.optimization_barrier((right_other, extra))
    right_all = jnp.where(
        first,
        jnp.concatenate([right_own, right_other], 1),
        jnp.concatenate([right_other, right_own], 1),
    )
    triangle = lax.dot_general(
        got[:, :rows].reshape(-1, tokens),
        right_all.reshape(-1, tokens),
        (((1,), (1,)), ((), ())),
        preferred_element_type=F32,
    ).astype(BF16)

    tri = lax.all_to_all(triangle.reshape(own, rows, tokens), CHIPS, 0, 0, tiled=True)
    payload = lax.ppermute(jnp.concatenate([tri, extra], 0), "yhi", SWAP)
    gate_value = jax.nn.sigmoid(per_row(out_gate.T, normed))

    tail = payload[own:].reshape(-1)
    weight_other = tail[: out_weight.size].reshape(out_weight.shape)
    scales_other = tail[out_weight.size : out_weight.size + 6 * own].reshape(3, 2, own)
    scales = jnp.concatenate(
        [jnp.stack([tri_gain, tri_bias]), jnp.sum(scales_other.astype(F32), 0)], 1
    )
    weight = jnp.concatenate([out_weight, weight_other], 0)
    weight = lax.dynamic_slice_in_dim(weight, half, own, 1)
    wide = jnp.concatenate([tri, payload[:own]], 0).astype(F32).reshape(2 * own, -1)
    onormed = normalise(wide, 0, scales[0], scales[1])
    projected = lax.dot_general(
        weight, onormed, (((0,), (0,)), ((), ())), preferred_element_type=F32
    )
    gate_value = gate_value.transpose(1, 0, 2).reshape(own, -1)
    updated = (gate_value * projected).astype(BF16)
    return updated.reshape(own, rows, tokens).transpose(1, 2, 0)


def solution(mesh):
    fine = Mesh(mesh.devices.reshape(4, 8, 2, 2, 2), RES + ("yhi",))
    placed = (
        P(RES, None, None),
        P(),
        P(),
        P(None, "yhi"),
        P(None, "yhi"),
        P(None, "yhi"),
        P(None, "yhi"),
        P("yhi"),
        P("yhi"),
        P("yhi", None),
        P(None, "yhi"),
    )
    return jax.shard_map(
        body, mesh=fine, in_specs=placed, out_specs=P(RES, None, "yhi"), check_vma=False
    )
```

time: 69.9 us -> 64.3 us (0.920)
  blocking collectives: 31.7 us -> 48.1 us
  waiting for transfers between devices: 16.7 us -> 6.43 us
  starting transfers between devices: 10.7 us -> 3.08 us
  other arithmetic: 5.57 us -> 1.08 us
    all_to_all x0 -> x1, blocking collectives: none -> 18.6 us  [body(): lax.all_to_all(triangle.reshape(own, rows, tokens), CHIPS, 0, 0, tiled=True)]
    all_to_all x1 -> x0, waiting for transfers between devices: 11.4 us -> none  [body(): lax.all_to_all(triangle.reshape(own, rows, tokens), CHIPS, 0, 0, tiled=True)]
    all_to_all x1 -> x0, starting transfers between devices: 7.1 us -> none  [body(): lax.all_to_all(triangle.reshape(own, rows, tokens), CHIPS, 0, 0, tiled=True)]
    reduce_sum x4, other arithmetic: 3.32 us -> 0.4 us  [the longest x2 0.3 us: normalise(): var = jnp.mean(centred * centred, axis, keepdims=True)]
    all_gather x1 -> x0, blocking collectives: 2.18 us -> none  [body(): lax.all_gather(got[:, rows:], 'core', axis=1, tiled=True)]
    convert_element_type x6 -> x4, other arithmetic: 1.84 us -> 0.32 us  [the longest x1 0.28 us: body(): left = (jax.nn.sigmoid(pre[:, :own]) * pre[:, own:2 * own]).astype(BF16)]
    ppermute x2, waiting for transfers between devices: 5.35 us -> 6.43 us  [the longest x1 5.13 us: body(): payload = lax.ppermute(jnp.concatenate([tri, extra], 0), 'yhi', SWAP)]
    unnamed x21 -> x24, local copies, waits for them, and re-layouts: 0.11 us -> 1.12 us
  transfers between devices with their start and end apart: 3 -> 2, of which waited for: 2 -> 2; matrix products, arithmetic and copies ran while one was open for 0% -> 1% of each run, Pallas kernels for 0% -> 0%
where the time goes in v3:
time: 64.3 us; the launch traced here: 64.1 us
  blocking collectives  48.1 us (75%)
  waiting for transfers between devices  6.43 us (10%)
  starting transfers between devices  3.08 us (5%)
  local copies, waits for them, and re-layouts  2.81 us (4%)
  matrix products  2.3 us (4%)
  other arithmetic  1.08 us (2%)
    all_to_all x1, blocking collectives, body(): got = lax.all_to_all(sent, CHIPS, 0, 0, tiled=True)  29.5 us
    all_to_all x1, blocking collectives, body(): lax.all_to_all(triangle.reshape(own, rows, tokens), CHIPS, 0, 0, tiled=True)  18.6 us
    ppermute x1, waiting for transfers between devices, body(): payload = lax.ppermute(jnp.concatenate([tri, extra], 0), 'yhi', SWAP)  5.13 us
    ppermute x1, starting transfers between devices, body(): payload = lax.ppermute(jnp.concatenate([tri, extra], 0), 'yhi', SWAP)  2.99 us
    ppermute x1, waiting for transfers between devices, body(): right_other = lax.ppermute(right_own, 'core', SWAP)  1.31 us
  transfers between devices with their start and end apart: 2, of which 2 were waited for; matrix products, arithmetic and copies ran while one was open for 1% of the time, Pallas kernels for 0%

profile of v3, /device:TPU:6, one launch (start us, length us, event | category | flops | bytes accessed | tf_op | source)
XLA Modules:
  0.0 64.1 jit_solution(2547320894811256585)
XLA Ops:
  0.1 1.0 %copy-done = bf16[4,512,128]{2,1,0:T(8,128)(2,1)S(1)} copy-done((bf16[4,512,128]{2,1,0:T(8,128)(2,1)S(1)}, bf16[4,512,128]{2,1,0:T(8,128)(2,1)}, u32[]{:S(2)}) %copy-start) | copy-done | bytes 524312
  1.0 0.3 fusion.50
  1.4 0.1 multiply_reduce_fusion
  1.6 0.5 fusion.32
  2.1 0.3 fusion.16
  2.5 0.3 copy.18
  2.8 29.5 %all_to_all.10 = bf16[64,8,512]{2,1,0:T(8,128)(2,1)S(1)} all-to-all(bf16[64,8,512]{2,1,0:T(8,128)(2,1)S(1)} %copy.18), channel_id=1, replica_groups=mesh['x'=4,'z'=8,'ylo'=2,'core'=2,'yhi'=2] {'x','z','ylo'}, dimensions={0} | all-to-all | bytes 1048576 | tf_op jit(solution)/shard_map/all_to_all | solution.py:60
  32.4 0.2 fusion.49
  32.6 0.1 collective-permute-start
  32.7 0.1 reshape.194
  32.9 1.3 %collective-permute-done = bf16[64,4,512]{2,1,0:T(4,128)(2,1)S(1)} collective-permute-done((bf16[64,4,512]{2,1,0:T(4,128)(2,1)S(1)}, bf16[64,4,512]{2,1,0:T(4,128)(2,1)S(1)}, u32[]{:S(2)}, u32[]{:S(2)}) %collective-permute-start) | collective-permute-done | bytes 262176 | tf_op jit(solution)/shard_map/ppermute | solution.py:65
  34.2 0.7 %convolution_convert_fusion = bf16[256,512]{1,0:T(8,128)(2,1)S(1)} fusion(bf16[256,512]{1,0:T(8,128)(2,1)S(1)} %reshape.192, bf16[64,4,512]{2,1,0:T(4,128)(2,1)S(1)} %collective-permute-done, bf16[64,4,512]{2,1,0:T(4,128)(2,1)S(1)} %get-tuple-element.26, pred[]{:T(512)S(6)} %eq.7), kind=kOutput, calls=%fused_computation.11 | convolution fusion | flops 136708096 | bytes 1048577 | tf_op jit(solution)/shard_map/dot_general | solution.py:75
  34.9 18.6 %all_to_all.11 = bf16[64,4,512]{2,1,0:T(4,128)(2,1)S(1)} all-to-all(bf16[64,4,512]{2,1,0:T(4,128)(2,1)S(1)} %reshape.196), channel_id=1, replica_groups=mesh['x'=4,'z'=8,'ylo'=2,'core'=2,'yhi'=2] {'x','z','ylo'}, dimensions={0} | all-to-all | bytes 524288 | tf_op jit(solution)/shard_map/all_to_all | solution.py:82
  53.5 0.2 pad_maximum_fusion.1
  53.7 3.0 %collective-permute-start.1 = (bf16[69,4,512]{2,1,0:T(4,128)(2,1)S(1)}, bf16[69,4,512]{2,1,0:T(4,128)(2,1)S(1)}, u32[]{:S(2)}, u32[]{:S(2)}) collective-permute-start(bf16[69,4,512]{2,1,0:T(4,128)(2,1)S(1)} %pad_maximum_fusion.1), channel_id=1, source_target_pairs={{0,1},{1,0},{2,3},{3,2},{4,5},{5,4},{6,7},{7,6},{8,9},{9,8},{10,11... | collective-permute-start | bytes 847880 | tf_op jit(solution)/shard_map/ppermute | solution.py:83
  56.7 0.4 fusion.6
  57.2 5.1 %collective-permute-done.1 = bf16[69,4,512]{2,1,0:T(4,128)(2,1)S(1)} collective-permute-done((bf16[69,4,512]{2,1,0:T(4,128)(2,1)S(1)}, bf16[69,4,512]{2,1,0:T(4,128)(2,1)S(1)}, u32[]{:S(2)}, u32[]{:S(2)}) %collective-permute-start.1) | collective-permute-done | bytes 282656 | tf_op jit(solution)/shard_map/ppermute | solution.py:83
  62.3 0.1 slice.59
  62.5 0.1 convert_reduce_fusion
  62.6 0.2 fusion.7
  62.8 0.1 slice.50
  62.9 0.1 pad_maximum_fusion.6
  63.0 0.4 fusion
  63.4 0.7 %copy.25 = bf16[8,4,8,512]{3,2,0,1:T(8,128)(2,1)} copy(bf16[8,4,8,512]{3,2,1,0:T(8,128)(2,1)S(1)} %bitcast.46) | data formatting | bytes 524288 | tf_op jit(solution)/shard_map/reshape | solution.py:101
  (43 shorter events, 0.5 us)
Async XLA Ops:
  0.0 1.0 %copy-start = (bf16[4,512,128]{2,1,0:T(8,128)(2,1)S(1)}, bf16[4,512,128]{2,1,0:T(8,128)(2,1)}, u32[]{:S(2)}) copy-start(bf16[4,512,128]{2,1,0:T(8,128)(2,1)} %param.11) | copy-start | bytes 1572868
  0.0 1.5 %copy-start.5 = (bf16[128,64]{0,1:T(8,128)(2,1)S(1)}, bf16[128,64]{0,1:T(8,128)(2,1)}, u32[]{:S(2)}) copy-start(bf16[128,64]{0,1:T(8,128)(2,1)} %param.15) | copy-start | bytes 49156
  0.0 1.5 %copy-start.4 = (bf16[128,64]{0,1:T(8,128)(2,1)S(1)}, bf16[128,64]{0,1:T(8,128)(2,1)}, u32[]{:S(2)}) copy-start(bf16[128,64]{0,1:T(8,128)(2,1)} %param.14) | copy-start | bytes 49156
  0.0 1.5 %copy-start.3 = (bf16[128,64]{0,1:T(8,128)(2,1)S(1)}, bf16[128,64]{0,1:T(8,128)(2,1)}, u32[]{:S(2)}) copy-start(bf16[128,64]{0,1:T(8,128)(2,1)} %param.17) | copy-start | bytes 49156
  0.0 1.5 %copy-start.2 = (bf16[128,64]{0,1:T(8,128)(2,1)S(1)}, bf16[128,64]{0,1:T(8,128)(2,1)}, u32[]{:S(2)}) copy-start(bf16[128,64]{0,1:T(8,128)(2,1)} %param.16) | copy-start | bytes 49156
  0.0 1.6 %copy-start.9 = (f32[128]{0:T(128)S(1)}, f32[128]{0:T(128)}, u32[]{:S(2)}) copy-start(f32[128]{0:T(128)} %param.12) | copy-start | bytes 1540
  0.0 1.6 %copy-start.8 = (f32[128]{0:T(128)S(1)}, f32[128]{0:T(128)}, u32[]{:S(2)}) copy-start(f32[128]{0:T(128)} %param.13) | copy-start | bytes 1540
  2.4 29.9 %copy-start.6 = (f32[64]{0:T(128)S(1)}, f32[64]{0:T(128)}, u32[]{:S(2)}) copy-start(f32[64]{0:T(128)} %param.19) | copy-start | bytes 772
  2.4 29.9 %copy-start.7 = (f32[64]{0:T(128)S(1)}, f32[64]{0:T(128)}, u32[]{:S(2)}) copy-start(f32[64]{0:T(128)} %param.18) | copy-start | bytes 772
  2.4 30.3 %copy-start.1 = (bf16[64,128]{1,0:T(8,128)(2,1)S(1)}, bf16[64,128]{1,0:T(8,128)(2,1)}, u32[]{:S(2)}) copy-start(bf16[64,128]{1,0:T(8,128)(2,1)} %param.20) | copy-start | bytes 49156
  32.6 1.6 %collective-permute-start = (bf16[64,4,512]{2,1,0:T(4,128)(2,1)S(1)}, bf16[64,4,512]{2,1,0:T(4,128)(2,1)S(1)}, u32[]{:S(2)}, u32[]{:S(2)}) collective-permute-start(bf16[64,4,512]{2,1,0:T(4,128)(2,1)S(1)} %get-tuple-element.26), channel_id=1, source_target_pairs={{0,2},{2,0},{1,3},{3,1},{4,6},{6,4},{5,7},{7,5},{8,10},{10,8},{9,1... | collective-permute-start | bytes 786440 | tf_op jit(solution)/shard_map/ppermute | solution.py:65
  32.9 23.8 %copy-start.10 = (bf16[128,64]{0,1:T(8,128)(2,1)S(1)}, bf16[128,64]{0,1:T(8,128)(2,1)}, u32[]{:S(2)}) copy-start(bf16[128,64]{0,1:T(8,128)(2,1)} %param.21) | copy-start | bytes 49156
  53.7 8.6 %collective-permute-start.1 = (bf16[69,4,512]{2,1,0:T(4,128)(2,1)S(1)}, bf16[69,4,512]{2,1,0:T(4,128)(2,1)S(1)}, u32[]{:S(2)}, u32[]{:S(2)}) collective-permute-start(bf16[69,4,512]{2,1,0:T(4,128)(2,1)S(1)} %pad_maximum_fusion.1), channel_id=1, source_target_pairs={{0,1},{1,0},{2,3},{3,2},{4,5},{5,4},{6,7},{7,6},{8,9},{9,8},{10,11... | collective-permute-start | bytes 847880 | tf_op jit(solution)/shard_map/ppermute | solution.py:83

commit v4 on v3

--- a/solution.py
+++ b/solution.py
@@ -1,6 +1,8 @@
 import jax
 import jax.numpy as jnp
 from jax import lax
+from jax.experimental import pallas as pl
+from jax.experimental.pallas import tpu as pltpu
 from jax.sharding import Mesh, PartitionSpec as P
 
 F32 = jnp.float32
@@ -29,6 +31,65 @@
     return lax.dot_general(matrix, values, (((2,), (1,)), ((0,), (0,))), preferred_element_type=F32)
 
 
+def pack(weight, scales):
+    pieces = jnp.pad(split3(scales).transpose(1, 0, 2).reshape(6, -1), ((0, 2), (0, 0)))
+    beside = jnp.concatenate([pieces[None], jnp.zeros((7,) + pieces.shape, BF16)], 0)
+    tiles = jnp.concatenate([weight.reshape(8, 8, -1), beside], 2)
+    return tiles.reshape(2, 4, 8, -1).transpose(0, 2, 1, 3).reshape(16, -1)
+
+
+def unpack(block):
+    tiles = [block[8 * g : 8 * g + 8, 128 * t : 128 * t + 128] for g in range(2) for t in range(4)]
+    half = tiles[0].shape[1] // 2
+    columns = tiles[0].astype(F32).T[half:]
+    gain = columns[:, 0:1] + columns[:, 1:2] + columns[:, 2:3]
+    bias = columns[:, 3:4] + columns[:, 4:5] + columns[:, 5:6]
+    return jnp.concatenate([tile[:, :half] for tile in tiles], 0), gain, bias
+
+
+def finish_kernel(mine_ref, other_ref, gate_ref, out_ref, done, sems):
+    rows, own, _ = gate_ref.shape
+    size = rows * own
+    weight, gain, bias = unpack(mine_ref[size:])
+    weight_other, gain_other, bias_other = unpack(other_ref[size:])
+    weight = jnp.concatenate([weight, weight_other], 1)
+    copies = [pltpu.make_async_copy(done.at[i], out_ref.at[i], sems.at[i]) for i in range(rows)]
+    width = 512
+    for i in range(rows):
+        for part in range(done.shape[2] // width):
+            at = slice(part * width, (part + 1) * width)
+            mine = mine_ref[i * own : (i + 1) * own, at].astype(F32)
+            other = other_ref[i * own : (i + 1) * own, at].astype(F32)
+            mean = (jnp.sum(mine, 0, keepdims=True) + jnp.sum(other, 0, keepdims=True)) / (2 * own)
+            mine, other = mine - mean, other - mean
+            square = jnp.sum(mine * mine + other * other, 0, keepdims=True)
+            root = lax.rsqrt(square / (2 * own) + EPS)
+            onormed = [mine * root * gain + bias, other * root * gain_other + bias_other]
+            onormed = jnp.concatenate(onormed, 0).astype(BF16)
+            projected = jnp.dot(weight, onormed, preferred_element_type=F32)
+            done[i, :, at] = (gate_ref[i, :, at] * projected).astype(BF16)
+        if 'each' == "each":
+            copies[i].start()
+        elif i % 2 == 1:
+            copies[i - 1].start()
+            copies[i].start()
+    for copy in copies:
+        copy.wait()
+
+
+def finish(mine, other, gate_value):
+    rows, own, tokens = gate_value.shape
+    operands = [pltpu.with_memory_space_constraint(a, pltpu.VMEM) for a in (mine, other, gate_value)]
+    return pl.pallas_call(
+        finish_kernel,
+        in_specs=[pl.BlockSpec(memory_space=pltpu.VMEM)] * 3,
+        out_specs=pl.BlockSpec(memory_space=pl.ANY),
+        out_shape=jax.ShapeDtypeStruct((rows, own, tokens), BF16),
+        scratch_shapes=[pltpu.VMEM((rows, own, tokens), BF16), pltpu.SemaphoreType.DMA((rows,))],
+        name="finish",
+    )(*operands)
+
+
 def body(
     pair,
     norm_gain,
@@ -54,8 +115,8 @@
     right = (jax.nn.sigmoid(pre[:, 2 * own : 3 * own]) * pre[:, 3 * own :]).astype(BF16)
     sent = jnp.concatenate([left, right], 0).transpose(1, 0, 2)
     first = lax.axis_index("core") == 0
-    half = lax.axis_index("yhi") * own
-    sent, first, half = lax.optimization_barrier((sent, first, half))
+    low = lax.axis_index("yhi") == 0
+    sent, first, low = lax.optimization_barrier((sent, first, low))
 
     got = lax.all_to_all(sent, CHIPS, 0, 0, tiled=True)
     got, out_weight, tri_gain, tri_bias = lax.optimization_barrier(
@@ -63,10 +124,11 @@
     )
     right_own = got[:, rows:]
     right_other = lax.ppermute(right_own, "core", SWAP)
-    extra = split3(jnp.stack([tri_gain, tri_bias]))
-    extra = jnp.concatenate([out_weight.reshape(-1), extra.reshape(-1)])
-    extra = jnp.pad(extra, (0, -extra.size % (rows * tokens))).reshape(-1, rows, tokens)
-    right_other, extra = lax.optimization_barrier((right_other, extra))
+    columns = out_weight.T.reshape(2, own, own)
+    scales = jnp.stack([tri_gain, tri_bias])
+    extra = pack(jnp.where(low, columns[1], columns[0]), scales)
+    extra_own = pack(jnp.where(low, columns[0], columns[1]), scales)
+    right_other, extra, extra_own = lax.optimization_barrier((right_other, extra, extra_own))
     right_all = jnp.where(
         first,
         jnp.concatenate([right_own, right_other], 1),
@@ -80,25 +142,11 @@
     ).astype(BF16)
 
     tri = lax.all_to_all(triangle.reshape(own, rows, tokens), CHIPS, 0, 0, tiled=True)
-    payload = lax.ppermute(jnp.concatenate([tri, extra], 0), "yhi", SWAP)
+    tri = tri.transpose(1, 0, 2).reshape(-1, tokens)
+    other = lax.ppermute(jnp.concatenate([tri, extra], 0), "yhi", SWAP)
     gate_value = jax.nn.sigmoid(per_row(out_gate.T, normed))
-
-    tail = payload[own:].reshape(-1)
-    weight_other = tail[: out_weight.size].reshape(out_weight.shape)
-    scales_other = tail[out_weight.size : out_weight.size + 6 * own].reshape(3, 2, own)
-    scales = jnp.concatenate(
-        [jnp.stack([tri_gain, tri_bias]), jnp.sum(scales_other.astype(F32), 0)], 1
-    )
-    weight = jnp.concatenate([out_weight, weight_other], 0)
-    weight = lax.dynamic_slice_in_dim(weight, half, own, 1)
-    wide = jnp.concatenate([tri, payload[:own]], 0).astype(F32).reshape(2 * own, -1)
-    onormed = normalise(wide, 0, scales[0], scales[1])
-    projected = lax.dot_general(
-        weight, onormed, (((0,), (0,)), ((), ())), preferred_element_type=F32
-    )
-    gate_value = gate_value.transpose(1, 0, 2).reshape(own, -1)
-    updated = (gate_value * projected).astype(BF16)
-    return updated.reshape(own, rows, tokens).transpose(1, 2, 0)
+    updated = finish(jnp.concatenate([tri, extra_own], 0), other, gate_value)
+    return updated.transpose(0, 2, 1)
 
 
 def solution(mesh):

time: 64.3 us -> 63.9 us (level)
  Pallas kernels: 0 us -> 1.37 us
  local copies, waits for them, and re-layouts: 2.81 us -> 1.82 us
    pallas_call x0 -> x1, Pallas kernels: none -> 1.37 us  [finish(): pl.pallas_call(finish_kernel, in_specs=[pl.BlockSpec(memory_space=pltpu.V...]
    reshape x5 -> x1, local copies, waits for them, and re-layouts: 0.88 us -> 0.02 us  [pack(): split3(scales).transpose(1, 0, 2).reshape(6, -1)]
where the time goes in v4:
time: 63.9 us; the launch traced here: 63.7 us
  blocking collectives  48.1 us (75%)
  waiting for transfers between devices  6.49 us (10%)
  starting transfers between devices  3.08 us (5%)
  matrix products  1.9 us (3%)
  local copies, waits for them, and re-layouts  1.82 us (3%)
  Pallas kernels  1.37 us (2%)
  other arithmetic  0.67 us (1%)
    all_to_all x1, blocking collectives, body(): got = lax.all_to_all(sent, CHIPS, 0, 0, tiled=True)  29.5 us
    all_to_all x1, blocking collectives, body(): lax.all_to_all(triangle.reshape(own, rows, tokens), CHIPS, 0, 0, tiled=True)  18.6 us
    ppermute x1, waiting for transfers between devices, body(): other = lax.ppermute(jnp.concatenate([tri, extra], 0), 'yhi', SWAP)  5.15 us
    ppermute x1, starting transfers between devices, body(): other = lax.ppermute(jnp.concatenate([tri, extra], 0), 'yhi', SWAP)  2.99 us
    pallas_call x1, Pallas kernels, finish(): pl.pallas_call(finish_kernel, in_specs=[pl.BlockSpec(memory_space=pltpu.V...  1.37 us
    ppermute x1, waiting for transfers between devices, body(): right_other = lax.ppermute(right_own, 'core', SWAP)  1.34 us
  transfers between devices with their start and end apart: 2, of which 2 were waited for; matrix products, arithmetic and copies ran while one was open for 1% of the time, Pallas kernels for 0%

profile of v4, /device:TPU:6, one launch (start us, length us, event | category | flops | bytes accessed | tf_op | source)
XLA Modules:
  0.0 63.7 jit_solution(17233434283544067217)
XLA Ops:
  0.0 0.0 copy-start
  0.1 1.0 %copy-done = bf16[4,512,128]{2,1,0:T(8,128)(2,1)S(1)} copy-done((bf16[4,512,128]{2,1,0:T(8,128)(2,1)S(1)}, bf16[4,512,128]{2,1,0:T(8,128)(2,1)}, u32[]{:S(2)}) %copy-start) | copy-done | bytes 524312
  1.0 0.3 fusion.30
  1.4 0.1 multiply_reduce_fusion
  1.6 0.5 fusion.20
  2.1 0.3 fusion.8
  2.4 0.0 copy-start.8
  2.4 0.0 copy-start.9
  2.4 0.0 copy-start.1
  2.5 0.3 copy.20
  2.8 29.5 %all_to_all.10 = bf16[64,8,512]{2,1,0:T(8,128)(2,1)S(1)} all-to-all(bf16[64,8,512]{2,1,0:T(8,128)(2,1)S(1)} %copy.20), channel_id=1, replica_groups=mesh['x'=4,'z'=8,'ylo'=2,'core'=2,'yhi'=2] {'x','z','ylo'}, dimensions={0} | all-to-all | bytes 1048576 | tf_op jit(solution)/shard_map/all_to_all | solution.py:121
  32.4 0.1 copy.21
  32.6 0.2 fusion.29
  32.8 0.1 collective-permute-start
  32.9 0.1 reshape.178
  33.0 0.1 maximum_bitcast_fusion.2
  33.0 1.3 %collective-permute-done = bf16[64,4,512]{2,1,0:T(4,128)(2,1)S(1)} collective-permute-done((bf16[64,4,512]{2,1,0:T(4,128)(2,1)S(1)}, bf16[64,4,512]{2,1,0:T(4,128)(2,1)S(1)}, u32[]{:S(2)}, u32[]{:S(2)}) %collective-permute-start) | collective-permute-done | bytes 262176 | tf_op jit(solution)/shard_map/ppermute | solution.py:126
  34.4 0.7 %convolution_convert_fusion = bf16[256,512]{1,0:T(8,128)(2,1)S(1)} fusion(bf16[256,512]{1,0:T(8,128)(2,1)S(1)} %reshape.178, bf16[64,4,512]{2,1,0:T(4,128)(2,1)S(1)} %collective-permute-done, bf16[64,4,512]{2,1,0:T(4,128)(2,1)S(1)} %get-tuple-element.28, pred[]{:T(512)S(6)} %eq.10), kind=kOutput, calls=%fused_computation.5 | convolution fusion | flops 136708096 | bytes 1048577 | tf_op jit(solution)/shard_map/dot_general | solution.py:137
  35.1 0.1 reshape.182
  35.1 18.6 %all_to_all.11 = bf16[64,4,512]{2,1,0:T(4,128)(2,1)S(1)} all-to-all(bf16[64,4,512]{2,1,0:T(4,128)(2,1)S(1)} %reshape.182), channel_id=1, replica_groups=mesh['x'=4,'z'=8,'ylo'=2,'core'=2,'yhi'=2] {'x','z','ylo'}, dimensions={0} | all-to-all | bytes 524288 | tf_op jit(solution)/shard_map/all_to_all | solution.py:144
  53.8 3.0 %collective-permute-start.1 = (bf16[272,512]{1,0:T(8,128)(2,1)S(1)}, bf16[272,512]{1,0:T(8,128)(2,1)S(1)}, u32[]{:S(2)}, u32[]{:S(2)}) collective-permute-start(bf16[272,512]{1,0:T(8,128)(2,1)S(1)} %get-tuple-element.29), channel_id=1, source_target_pairs={{0,1},{1,0},{2,3},{3,2},{4,5},{5,4},{6,7},{7,6},{8,9},{9,8},{10,11... | collective-permute-start | bytes 835592 | tf_op jit(solution)/shard_map/ppermute | solution.py:146
  56.8 0.4 fusion.3.gate_ref
  57.2 5.1 %collective-permute-done.1.other_ref = bf16[272,512]{1,0:T(8,128)(2,1)S(1)} collective-permute-done((bf16[272,512]{1,0:T(8,128)(2,1)S(1)}, bf16[272,512]{1,0:T(8,128)(2,1)S(1)}, u32[]{:S(2)}, u32[]{:S(2)}) %collective-permute-start.1) | collective-permute-done | bytes 278560 | tf_op jit(solution)/shard_map/ppermute | solution.py:146
  62.4 1.4 %finish.1 = bf16[4,64,512]{2,1,0:T(8,128)(2,1)} custom-call(bf16[272,512]{1,0:T(8,128)(2,1)S(1)} %get-tuple-element.30.mine_ref, bf16[272,512]{1,0:T(8,128)(2,1)S(1)} %collective-permute-done.1.other_ref, f32[4,64,512]{2,1,0:T(8,128)S(1)} %fusion.3.gate_ref), custom_call_target="tpu_custom_call" | custom-call | tf_op jit(solution)/shard_map/finish/pallas_call | solution.py:83
  (32 shorter events, 0.3 us)
Async XLA Ops:
  0.0 1.0 %copy-start = (bf16[4,512,128]{2,1,0:T(8,128)(2,1)S(1)}, bf16[4,512,128]{2,1,0:T(8,128)(2,1)}, u32[]{:S(2)}) copy-start(bf16[4,512,128]{2,1,0:T(8,128)(2,1)} %param.11) | copy-start | bytes 1572868
  0.0 1.5 %copy-start.5 = (bf16[128,64]{0,1:T(8,128)(2,1)S(1)}, bf16[128,64]{0,1:T(8,128)(2,1)}, u32[]{:S(2)}) copy-start(bf16[128,64]{0,1:T(8,128)(2,1)} %param.15) | copy-start | bytes 49156
  0.0 1.5 %copy-start.4 = (bf16[128,64]{0,1:T(8,128)(2,1)S(1)}, bf16[128,64]{0,1:T(8,128)(2,1)}, u32[]{:S(2)}) copy-start(bf16[128,64]{0,1:T(8,128)(2,1)} %param.14) | copy-start | bytes 49156
  0.0 1.5 %copy-start.3 = (bf16[128,64]{0,1:T(8,128)(2,1)S(1)}, bf16[128,64]{0,1:T(8,128)(2,1)}, u32[]{:S(2)}) copy-start(bf16[128,64]{0,1:T(8,128)(2,1)} %param.17) | copy-start | bytes 49156
  0.0 1.5 %copy-start.2 = (bf16[128,64]{0,1:T(8,128)(2,1)S(1)}, bf16[128,64]{0,1:T(8,128)(2,1)}, u32[]{:S(2)}) copy-start(bf16[128,64]{0,1:T(8,128)(2,1)} %param.16) | copy-start | bytes 49156
  0.0 1.6 %copy-start.7 = (f32[128]{0:T(128)S(1)}, f32[128]{0:T(128)}, u32[]{:S(2)}) copy-start(f32[128]{0:T(128)} %param.12) | copy-start | bytes 1540
  0.0 1.6 %copy-start.6 = (f32[128]{0:T(128)S(1)}, f32[128]{0:T(128)}, u32[]{:S(2)}) copy-start(f32[128]{0:T(128)} %param.13) | copy-start | bytes 1540
  2.4 29.9 %copy-start.8 = (f32[64]{0:T(128)S(1)}, f32[64]{0:T(128)}, u32[]{:S(2)}) copy-start(f32[64]{0:T(128)} %param.19) | copy-start | bytes 772
  2.4 29.9 %copy-start.9 = (f32[64]{0:T(128)S(1)}, f32[64]{0:T(128)}, u32[]{:S(2)}) copy-start(f32[64]{0:T(128)} %param.18) | copy-start | bytes 772
  2.4 30.0 %copy-start.1 = (bf16[64,128]{1,0:T(8,128)(2,1)S(1)}, bf16[64,128]{1,0:T(8,128)(2,1)}, u32[]{:S(2)}) copy-start(bf16[64,128]{1,0:T(8,128)(2,1)} %param.20) | copy-start | bytes 49156
  32.8 1.6 %collective-permute-start = (bf16[64,4,512]{2,1,0:T(4,128)(2,1)S(1)}, bf16[64,4,512]{2,1,0:T(4,128)(2,1)S(1)}, u32[]{:S(2)}, u32[]{:S(2)}) collective-permute-start(bf16[64,4,512]{2,1,0:T(4,128)(2,1)S(1)} %get-tuple-element.28), channel_id=1, source_target_pairs={{0,2},{2,0},{1,3},{3,1},{4,6},{6,4},{5,7},{7,5},{8,10},{10,8},{9,1... | collective-permute-start | bytes 786440 | tf_op jit(solution)/shard_map/ppermute | solution.py:126
  34.4 22.4 %copy-start.10 = (bf16[128,64]{0,1:T(8,128)(2,1)S(1)}, bf16[128,64]{0,1:T(8,128)(2,1)}, u32[]{:S(2)}) copy-start(bf16[128,64]{0,1:T(8,128)(2,1)} %param.21) | copy-start | bytes 49156
  53.8 8.6 %collective-permute-start.1 = (bf16[272,512]{1,0:T(8,128)(2,1)S(1)}, bf16[272,512]{1,0:T(8,128)(2,1)S(1)}, u32[]{:S(2)}, u32[]{:S(2)}) collective-permute-start(bf16[272,512]{1,0:T(8,128)(2,1)S(1)} %get-tuple-element.29), channel_id=1, source_target_pairs={{0,1},{1,0},{2,3},{3,2},{4,5},{5,4},{6,7},{7,6},{8,9},{9,8},{10,11... | collective-permute-start | bytes 835592 | tf_op jit(solution)/shard_map/ppermute | solution.py:146

commit v5 on v4

--- a/solution.py
+++ b/solution.py
@@ -13,17 +13,11 @@
 SWAP = [(0, 1), (1, 0)]
 
 
-def normalise(values, axis, gain, bias):
-    centred = values - jnp.mean(values, axis, keepdims=True)
-    var = jnp.mean(centred * centred, axis, keepdims=True)
-    return (centred * lax.rsqrt(var + EPS) * gain[:, None] + bias[:, None]).astype(BF16)
-
-
 def split3(values):
     high = values.astype(BF16)
     rest = values - high.astype(F32)
     middle = rest.astype(BF16)
-    return jnp.stack([high, middle, (rest - middle.astype(F32)).astype(BF16)])
+    return [high, middle, (rest - middle.astype(F32)).astype(BF16)]
 
 
 def per_row(matrix, values):
@@ -31,20 +25,100 @@
     return lax.dot_general(matrix, values, (((2,), (1,)), ((0,), (0,))), preferred_element_type=F32)
 
 
+def sigmoid(values):
+    return 0.5 * jnp.tanh(0.5 * values) + 0.5
+
+
 def pack(weight, scales):
-    pieces = jnp.pad(split3(scales).transpose(1, 0, 2).reshape(6, -1), ((0, 2), (0, 0)))
-    beside = jnp.concatenate([pieces[None], jnp.zeros((7,) + pieces.shape, BF16)], 0)
-    tiles = jnp.concatenate([weight.reshape(8, 8, -1), beside], 2)
-    return tiles.reshape(2, 4, 8, -1).transpose(0, 2, 1, 3).reshape(16, -1)
+    pieces = [piece.astype(F32) for row in scales for piece in split3(row)]
+    beside = jnp.concatenate(pieces + [jnp.zeros_like(pieces[0])] * 2, 0)
+    tiles = [
+        jnp.concatenate([weight[8 * g : 8 * g + 8], beside if g == 0 else jnp.zeros_like(beside)], 1)
+        for g in range(8)
+    ]
+    halves = [jnp.concatenate(tiles[4 * h : 4 * h + 4], 1) for h in range(2)]
+    return jnp.concatenate(halves, 0).astype(BF16)
+
+
+def project_kernel(*refs):
+    pair_ref, scale_refs, weight_refs, out_weight_ref = refs[0], refs[1:5], refs[5:9], refs[9]
+    sent_ref, normed_ref, extra_ref, extra_own_ref = refs[10:14]
+    pair_buf, scale_buf, tri_buf, weight_buf, out_weight_buf, sem, sems = refs[14:]
+    rows, tokens, channels = pair_buf.shape
+    own = weight_refs[0].shape[0]
+    load = pltpu.make_async_copy(pair_ref, pair_buf, sem)
+    load.start()
+    copies = [pltpu.make_async_copy(out_weight_ref, out_weight_buf, sems.at[8])]
+    for n in range(4):
+        place = (scale_buf, tri_buf)[n // 2].at[pl.ds(8 * (n % 2), 1)]
+        copies.append(pltpu.make_async_copy(scale_refs[n], place, sems.at[n]))
+        place = weight_buf.at[pl.ds(own * n, own)]
+        copies.append(pltpu.make_async_copy(weight_refs[n], place, sems.at[4 + n]))
+    for copy in copies:
+        copy.start()
+    for copy in copies + [load]:
+        copy.wait()
+
+    scales = scale_buf[...].T
+    values = pair_buf[...].reshape(rows * tokens, channels).T.astype(F32)
+    centred = values - jnp.mean(values, 0, keepdims=True)
+    var = jnp.mean(centred * centred, 0, keepdims=True)
+    normed = centred * lax.rsqrt(var + EPS) * scales[:, 0:1] + scales[:, 8:9]
+    normed = normed.astype(BF16)
+    pre = jnp.dot(weight_buf[...], normed, preferred_element_type=F32)
+    for i in range(rows):
+        at = slice(i * tokens, (i + 1) * tokens)
+        normed_ref[i] = normed[:, at]
+        sent_ref[i] = (sigmoid(pre[:own, at]) * pre[own : 2 * own, at]).astype(BF16)
+        right = sigmoid(pre[2 * own : 3 * own, at]) * pre[3 * own :, at]
+        sent_ref[rows + i] = right.astype(BF16)
+
+    tri = [tri_buf[0:1], tri_buf[8:9]]
+    columns = out_weight_buf[...].astype(F32).T
+    low = lax.axis_index("yhi") == 0
+    extra_ref[...] = pack(jnp.where(low, columns[own:], columns[:own]), tri)
+    extra_own_ref[...] = pack(jnp.where(low, columns[:own], columns[own:]), tri)
+
+
+def project(pair, scales, weights, out_weight):
+    rows, tokens, channels = pair.shape
+    own = weights[0].shape[0]
+    return pl.pallas_call(
+        project_kernel,
+        in_specs=[pl.BlockSpec(memory_space=pl.ANY)] * 10,
+        out_specs=[pl.BlockSpec(memory_space=pltpu.VMEM)] * 4,
+        out_shape=[
+            pltpu.VMEM((2 * rows, own, tokens), BF16),
+            pltpu.VMEM((rows, channels, tokens), BF16),
+            pltpu.VMEM((16, 512), BF16),
+            pltpu.VMEM((16, 512), BF16),
+        ],
+        scratch_shapes=[
+            pltpu.VMEM((rows, tokens, channels), BF16),
+            pltpu.VMEM((16, channels), F32),
+            pltpu.VMEM((16, own), F32),
+            pltpu.VMEM((4 * own, channels), BF16),
+            pltpu.VMEM((own, channels), BF16),
+            pltpu.SemaphoreType.DMA,
+            pltpu.SemaphoreType.DMA((9,)),
+        ],
+        name="project",
+    )(
+        *[
+            pltpu.with_memory_space_constraint(a, pltpu.HBM)
+            for a in [pair] + [v[None] for v in scales] + weights + [out_weight]
+        ]
+    )
 
 
 def unpack(block):
+    block = block.astype(F32)
     tiles = [block[8 * g : 8 * g + 8, 128 * t : 128 * t + 128] for g in range(2) for t in range(4)]
     half = tiles[0].shape[1] // 2
-    columns = tiles[0].astype(F32).T[half:]
+    columns = tiles[0].T[half:]
     gain = columns[:, 0:1] + columns[:, 1:2] + columns[:, 2:3]
     bias = columns[:, 3:4] + columns[:, 4:5] + columns[:, 5:6]
-    return jnp.concatenate([tile[:, :half] for tile in tiles], 0), gain, bias
+    return jnp.concatenate([tile[:, :half] for tile in tiles], 0).astype(BF16), gain, bias
 
 
 def finish_kernel(mine_ref, other_ref, gate_ref, out_ref, done, sems):
@@ -106,29 +180,19 @@
     rows, tokens, channels = pair.shape
     own = left_weight.shape[1]
 
-    eye = jnp.broadcast_to(jnp.eye(channels, dtype=BF16), (rows, channels, channels))
-    wide = lax.dot_general(eye, pair, (((2,), (2,)), ((0,), (0,))), preferred_element_type=F32)
-    normed = normalise(wide, 1, norm_gain, norm_bias)
-    weights = [left_gate.T, left_weight.T, right_gate.T, right_weight.T]
-    pre = per_row(jnp.concatenate(weights, 0), normed)
-    left = (jax.nn.sigmoid(pre[:, :own]) * pre[:, own : 2 * own]).astype(BF16)
-    right = (jax.nn.sigmoid(pre[:, 2 * own : 3 * own]) * pre[:, 3 * own :]).astype(BF16)
-    sent = jnp.concatenate([left, right], 0).transpose(1, 0, 2)
+    sent, normed, extra, extra_own = project(
+        pair,
+        [norm_gain, norm_bias, tri_gain, tri_bias],
+        [left_gate.T, left_weight.T, right_gate.T, right_weight.T],
+        out_weight,
+    )
+    sent = sent.transpose(1, 0, 2)
     first = lax.axis_index("core") == 0
-    low = lax.axis_index("yhi") == 0
-    sent, first, low = lax.optimization_barrier((sent, first, low))
+    sent, first = lax.optimization_barrier((sent, first))
 
     got = lax.all_to_all(sent, CHIPS, 0, 0, tiled=True)
-    got, out_weight, tri_gain, tri_bias = lax.optimization_barrier(
-        (got, out_weight, tri_gain, tri_bias)
-    )
     right_own = got[:, rows:]
     right_other = lax.ppermute(right_own, "core", SWAP)
-    columns = out_weight.T.reshape(2, own, own)
-    scales = jnp.stack([tri_gain, tri_bias])
-    extra = pack(jnp.where(low, columns[1], columns[0]), scales)
-    extra_own = pack(jnp.where(low, columns[0], columns[1]), scales)
-    right_other, extra, extra_own = lax.optimization_barrier((right_other, extra, extra_own))
     right_all = jnp.where(
         first,
         jnp.concatenate([right_own, right_other], 1),

time: 63.9 us -> 63.3 us (level)
  Pallas kernels: 1.37 us -> 3.47 us
  local copies, waits for them, and re-layouts: 1.82 us -> 0.65 us
  matrix products: 1.9 us -> 0.96 us
    pallas_call x0 -> x1, Pallas kernels: none -> 2.1 us  [project(): pl.pallas_call(project_kernel, in_specs=[pl.BlockSpec(memory_space=pl.ANY...]
    unnamed x22 -> x2, local copies, waits for them, and re-layouts: 1.02 us -> 0.01 us
where the time goes in v5:
time: 63.3 us; the launch traced here: 63.1 us
  blocking collectives  48.1 us (76%)
  waiting for transfers between devices  6.72 us (11%)
  Pallas kernels  3.47 us (5%)
  starting transfers between devices  3.08 us (5%)
  matrix products  0.96 us (2%)
  local copies, waits for them, and re-layouts  0.65 us (1%)
    all_to_all x1, blocking collectives, body(): got = lax.all_to_all(sent, CHIPS, 0, 0, tiled=True)  29.5 us
    all_to_all x1, blocking collectives, body(): lax.all_to_all(triangle.reshape(own, rows, tokens), CHIPS, 0, 0, tiled=True)  18.6 us
    ppermute x1, waiting for transfers between devices, body(): other = lax.ppermute(jnp.concatenate([tri, extra], 0), 'yhi', SWAP)  5.27 us
    ppermute x1, starting transfers between devices, body(): other = lax.ppermute(jnp.concatenate([tri, extra], 0), 'yhi', SWAP)  2.98 us
    pallas_call x1, Pallas kernels, project(): pl.pallas_call(project_kernel, in_specs=[pl.BlockSpec(memory_space=pl.ANY...  2.1 us
    ppermute x1, waiting for transfers between devices, body(): right_other = lax.ppermute(right_own, 'core', SWAP)  1.45 us
    pallas_call x1, Pallas kernels, finish(): pl.pallas_call(finish_kernel, in_specs=[pl.BlockSpec(memory_space=pltpu.V...  1.36 us
  transfers between devices with their start and end apart: 2, of which 2 were waited for; matrix products, arithmetic and copies ran while one was open for 1% of the time, Pallas kernels for 0%

profile of v5, /device:TPU:6, one launch (start us, length us, event | category | flops | bytes accessed | tf_op | source)
XLA Modules:
  0.0 63.1 jit_solution(3219434720822998773)
XLA Ops:
  0.0 0.0 copy-start
  0.0 2.1 %project.1 = (bf16[8,64,512]{2,1,0:T(8,128)(2,1)S(1)}, bf16[4,128,512]{2,1,0:T(8,128)(2,1)S(1)}, bf16[16,512]{1,0:T(8,128)(2,1)S(1)}, bf16[16,512]{1,0:T(8,128)(2,1)S(1)}) custom-call(bf16[4,512,128]{2,1,0:T(8,128)(2,1)} %refs_0_.1, f32[1,128]{1,0:T(1,128)} %bitcast.28, f32[1,128]{1,0:T(1,128)} %bitcast.29, f32[1,64]{1,0:T(1,128)} %bitcast.30, ...), custom_call_target="tpu_custom_call" | custom-call | tf_op jit(solution)/shard_map/project/pallas_call | solution.py:86
  2.1 0.3 copy.16
  2.4 29.5 %all_to_all.10 = bf16[64,8,512]{2,1,0:T(8,128)(2,1)S(1)} all-to-all(bf16[64,8,512]{2,1,0:T(8,128)(2,1)S(1)} %copy.16), channel_id=1, replica_groups=mesh['x'=4,'z'=8,'ylo'=2,'core'=2,'yhi'=2] {'x','z','ylo'}, dimensions={0} | all-to-all | bytes 1048576 | tf_op jit(solution)/shard_map/all_to_all | solution.py:193
  31.9 0.2 fusion.14
  32.1 0.1 collective-permute-start
  32.2 0.1 reshape.22
  32.3 1.5 %collective-permute-done = bf16[64,4,512]{2,1,0:T(4,128)(2,1)S(1)} collective-permute-done((bf16[64,4,512]{2,1,0:T(4,128)(2,1)S(1)}, bf16[64,4,512]{2,1,0:T(4,128)(2,1)S(1)}, u32[]{:S(2)}, u32[]{:S(2)}) %collective-permute-start) | collective-permute-done | bytes 262176 | tf_op jit(solution)/shard_map/ppermute | solution.py:195
  33.7 0.7 %convolution_convert_fusion = bf16[256,512]{1,0:T(8,128)(2,1)S(1)} fusion(bf16[256,512]{1,0:T(8,128)(2,1)S(1)} %reshape.22, bf16[64,4,512]{2,1,0:T(4,128)(2,1)S(1)} %collective-permute-done, bf16[64,4,512]{2,1,0:T(4,128)(2,1)S(1)} %get-tuple-element.17, pred[]{:T(512)S(6)} %eq.3), kind=kOutput, calls=%fused_computation.5 | convolution fusion | flops 136708096 | bytes 1048577 | tf_op jit(solution)/shard_map/dot_general | solution.py:201
  34.4 0.1 reshape.23
  34.5 18.6 %all_to_all.11 = bf16[64,4,512]{2,1,0:T(4,128)(2,1)S(1)} all-to-all(bf16[64,4,512]{2,1,0:T(4,128)(2,1)S(1)} %reshape.23), channel_id=1, replica_groups=mesh['x'=4,'z'=8,'ylo'=2,'core'=2,'yhi'=2] {'x','z','ylo'}, dimensions={0} | all-to-all | bytes 524288 | tf_op jit(solution)/shard_map/all_to_all | solution.py:208
  53.2 3.0 %collective-permute-start.1 = (bf16[272,512]{1,0:T(8,128)(2,1)S(1)}, bf16[272,512]{1,0:T(8,128)(2,1)S(1)}, u32[]{:S(2)}, u32[]{:S(2)}) collective-permute-start(bf16[272,512]{1,0:T(8,128)(2,1)S(1)} %get-tuple-element.19), channel_id=1, source_target_pairs={{0,1},{1,0},{2,3},{3,2},{4,5},{5,4},{6,7},{7,6},{8,9},{9,8},{10,11... | collective-permute-start | bytes 835592 | tf_op jit(solution)/shard_map/ppermute | solution.py:210
  56.2 0.0 copy-done
  56.2 0.3 fusion.3.gate_ref
  56.5 5.3 %collective-permute-done.1.other_ref = bf16[272,512]{1,0:T(8,128)(2,1)S(1)} collective-permute-done((bf16[272,512]{1,0:T(8,128)(2,1)S(1)}, bf16[272,512]{1,0:T(8,128)(2,1)S(1)}, u32[]{:S(2)}, u32[]{:S(2)}) %collective-permute-start.1) | collective-permute-done | bytes 278560 | tf_op jit(solution)/shard_map/ppermute | solution.py:210
  61.7 1.4 %finish.1 = bf16[4,64,512]{2,1,0:T(8,128)(2,1)} custom-call(bf16[272,512]{1,0:T(8,128)(2,1)S(1)} %get-tuple-element.20.mine_ref, bf16[272,512]{1,0:T(8,128)(2,1)S(1)} %collective-permute-done.1.other_ref, f32[4,64,512]{2,1,0:T(8,128)S(1)} %fusion.3.gate_ref), custom_call_target="tpu_custom_call" | custom-call | tf_op jit(solution)/shard_map/finish/pallas_call | solution.py:157
  (2 shorter events, 0.1 us)
Async XLA Ops:
  0.0 56.2 %copy-start = (bf16[128,64]{0,1:T(8,128)(2,1)S(1)}, bf16[128,64]{0,1:T(8,128)(2,1)}, u32[]{:S(2)}) copy-start(bf16[128,64]{0,1:T(8,128)(2,1)} %param.21) | copy-start | bytes 49156
  32.1 1.6 %collective-permute-start = (bf16[64,4,512]{2,1,0:T(4,128)(2,1)S(1)}, bf16[64,4,512]{2,1,0:T(4,128)(2,1)S(1)}, u32[]{:S(2)}, u32[]{:S(2)}) collective-permute-start(bf16[64,4,512]{2,1,0:T(4,128)(2,1)S(1)} %get-tuple-element.17), channel_id=1, source_target_pairs={{0,2},{2,0},{1,3},{3,1},{4,6},{6,4},{5,7},{7,5},{8,10},{10,8},{9,1... | collective-permute-start | bytes 786440 | tf_op jit(solution)/shard_map/ppermute | solution.py:195
  53.2 8.6 %collective-permute-start.1 = (bf16[272,512]{1,0:T(8,128)(2,1)S(1)}, bf16[272,512]{1,0:T(8,128)(2,1)S(1)}, u32[]{:S(2)}, u32[]{:S(2)}) collective-permute-start(bf16[272,512]{1,0:T(8,128)(2,1)S(1)} %get-tuple-element.19), channel_id=1, source_target_pairs={{0,1},{1,0},{2,3},{3,2},{4,5},{5,4},{6,7},{7,6},{8,9},{9,8},{10,11... | collective-permute-start | bytes 835592 | tf_op jit(solution)/shard_map/ppermute | solution.py:210

commit v6 on v5

--- a/solution.py
+++ b/solution.py
@@ -29,15 +29,12 @@
     return 0.5 * jnp.tanh(0.5 * values) + 0.5
 
 
-def pack(weight, scales):
-    pieces = [piece.astype(F32) for row in scales for piece in split3(row)]
-    beside = jnp.concatenate(pieces + [jnp.zeros_like(pieces[0])] * 2, 0)
-    tiles = [
-        jnp.concatenate([weight[8 * g : 8 * g + 8], beside if g == 0 else jnp.zeros_like(beside)], 1)
-        for g in range(8)
-    ]
-    halves = [jnp.concatenate(tiles[4 * h : 4 * h + 4], 1) for h in range(2)]
-    return jnp.concatenate(halves, 0).astype(BF16)
+def pack(columns):
+    return jnp.concatenate([columns[16 * t : 16 * t + 16] for t in range(4)], 1).astype(BF16)
+
+
+def unpack(block):
+    return jnp.concatenate([block[:, 128 * t : 128 * t + 128] for t in range(4)], 0)
 
 
 def project_kernel(*refs):
@@ -69,15 +66,19 @@
     for i in range(rows):
         at = slice(i * tokens, (i + 1) * tokens)
         normed_ref[i] = normed[:, at]
-        sent_ref[i] = (sigmoid(pre[:own, at]) * pre[own : 2 * own, at]).astype(BF16)
+        sent_ref[rows + i] = (sigmoid(pre[:own, at]) * pre[own : 2 * own, at]).astype(BF16)
         right = sigmoid(pre[2 * own : 3 * own, at]) * pre[3 * own :, at]
-        sent_ref[rows + i] = right.astype(BF16)
-
-    tri = [tri_buf[0:1], tri_buf[8:9]]
+        sent_ref[i] = right.astype(BF16)
+
+    pieces = [piece.astype(F32) for n in (0, 8) for piece in split3(tri_buf[n : n + 1])]
+    pieces = jnp.concatenate(pieces + [jnp.zeros_like(pieces[0])] * 2, 0).T
+    blank = jnp.zeros((own, channels - own - 8), F32)
     columns = out_weight_buf[...].astype(F32).T
     low = lax.axis_index("yhi") == 0
-    extra_ref[...] = pack(jnp.where(low, columns[own:], columns[:own]), tri)
-    extra_own_ref[...] = pack(jnp.where(low, columns[:own], columns[own:]), tri)
+    mine = jnp.where(low, columns[:own], columns[own:])
+    theirs = jnp.where(low, columns[own:], columns[:own])
+    extra_ref[...] = pack(jnp.concatenate([pieces, blank, theirs], 1))
+    extra_own_ref[...] = pack(jnp.concatenate([mine, pieces, blank], 1))
 
 
 def project(pair, scales, weights, out_weight):
@@ -111,42 +112,32 @@
     )
 
 
-def unpack(block):
-    block = block.astype(F32)
-    tiles = [block[8 * g : 8 * g + 8, 128 * t : 128 * t + 128] for g in range(2) for t in range(4)]
-    half = tiles[0].shape[1] // 2
-    columns = tiles[0].T[half:]
-    gain = columns[:, 0:1] + columns[:, 1:2] + columns[:, 2:3]
-    bias = columns[:, 3:4] + columns[:, 4:5] + columns[:, 5:6]
-    return jnp.concatenate([tile[:, :half] for tile in tiles], 0).astype(BF16), gain, bias
+def scales_of(pieces):
+    gain = pieces[:, 0:1] + pieces[:, 1:2] + pieces[:, 2:3]
+    return gain, pieces[:, 3:4] + pieces[:, 4:5] + pieces[:, 5:6]
 
 
 def finish_kernel(mine_ref, other_ref, gate_ref, out_ref, done, sems):
     rows, own, _ = gate_ref.shape
     size = rows * own
-    weight, gain, bias = unpack(mine_ref[size:])
-    weight_other, gain_other, bias_other = unpack(other_ref[size:])
-    weight = jnp.concatenate([weight, weight_other], 1)
+    columns, columns_other = unpack(mine_ref[size:]), unpack(other_ref[size:])
+    lane = lax.broadcasted_iota(jnp.int32, columns.shape, 1)
+    weight = jnp.where(lane < own, columns.astype(F32), columns_other.astype(F32)).astype(BF16)
+    gain, bias = scales_of(columns[:, own : own + 8].astype(F32))
+    gain_other, bias_other = scales_of(columns_other[:, 0:8].astype(F32))
     copies = [pltpu.make_async_copy(done.at[i], out_ref.at[i], sems.at[i]) for i in range(rows)]
-    width = 512
     for i in range(rows):
-        for part in range(done.shape[2] // width):
-            at = slice(part * width, (part + 1) * width)
-            mine = mine_ref[i * own : (i + 1) * own, at].astype(F32)
-            other = other_ref[i * own : (i + 1) * own, at].astype(F32)
-            mean = (jnp.sum(mine, 0, keepdims=True) + jnp.sum(other, 0, keepdims=True)) / (2 * own)
-            mine, other = mine - mean, other - mean
-            square = jnp.sum(mine * mine + other * other, 0, keepdims=True)
-            root = lax.rsqrt(square / (2 * own) + EPS)
-            onormed = [mine * root * gain + bias, other * root * gain_other + bias_other]
-            onormed = jnp.concatenate(onormed, 0).astype(BF16)
-            projected = jnp.dot(weight, onormed, preferred_element_type=F32)
-            done[i, :, at] = (gate_ref[i, :, at] * projected).astype(BF16)
-        if 'each' == "each":
-            copies[i].start()
-        elif i % 2 == 1:
-            copies[i - 1].start()
-            copies[i].start()
+        mine = mine_ref[i * own : (i + 1) * own].astype(F32)
+        other = other_ref[i * own : (i + 1) * own].astype(F32)
+        mean = (jnp.sum(mine, 0, keepdims=True) + jnp.sum(other, 0, keepdims=True)) / (2 * own)
+        mine, other = mine - mean, other - mean
+        square = jnp.sum(mine * mine + other * other, 0, keepdims=True)
+        root = lax.rsqrt(square / (2 * own) + EPS)
+        onormed = [mine * root * gain + bias, other * root * gain_other + bias_other]
+        onormed = jnp.concatenate(onormed, 0).astype(BF16)
+        projected = jnp.dot(weight, onormed, preferred_element_type=F32)
+        done[i] = (gate_ref[i] * projected).astype(BF16)
+        copies[i].start()
     for copy in copies:
         copy.wait()
 
@@ -191,7 +182,7 @@
     sent, first = lax.optimization_barrier((sent, first))
 
     got = lax.all_to_all(sent, CHIPS, 0, 0, tiled=True)
-    right_own = got[:, rows:]
+    right_own, got = lax.optimization_barrier((got[:, :rows], got))
     right_other = lax.ppermute(right_own, "core", SWAP)
     right_all = jnp.where(
         first,
@@ -199,7 +190,7 @@
         jnp.concatenate([right_other, right_own], 1),
     )
     triangle = lax.dot_general(
-        got[:, :rows].reshape(-1, tokens),
+        got[:, rows:].reshape(-1, tokens),
         right_all.reshape(-1, tokens),
         (((1,), (1,)), ((), ())),
         preferred_element_type=F32,

time: 63.3 us -> 63.1 us (level)
  no operation moved by 1% of the time
where the time goes in v6:
time: 63.1 us; the launch traced here: 62.9 us
  blocking collectives  48.1 us (76%)
  waiting for transfers between devices  6.56 us (10%)
  Pallas kernels  3.38 us (5%)
  starting transfers between devices  3.08 us (5%)
  matrix products  0.96 us (2%)
  local copies, waits for them, and re-layouts  0.7 us (1%)
    all_to_all x1, blocking collectives, body(): got = lax.all_to_all(sent, CHIPS, 0, 0, tiled=True)  29.5 us
    all_to_all x1, blocking collectives, body(): lax.all_to_all(triangle.reshape(own, rows, tokens), CHIPS, 0, 0, tiled=True)  18.6 us
    ppermute x1, waiting for transfers between devices, body(): other = lax.ppermute(jnp.concatenate([tri, extra], 0), 'yhi', SWAP)  5.25 us
    ppermute x1, starting transfers between devices, body(): other = lax.ppermute(jnp.concatenate([tri, extra], 0), 'yhi', SWAP)  2.99 us
    pallas_call x1, Pallas kernels, project(): pl.pallas_call(project_kernel, in_specs=[pl.BlockSpec(memory_space=pl.ANY...  2.1 us
    ppermute x1, waiting for transfers between devices, body(): right_other = lax.ppermute(right_own, 'core', SWAP)  1.3 us
    pallas_call x1, Pallas kernels, finish(): pl.pallas_call(finish_kernel, in_specs=[pl.BlockSpec(memory_space=pltpu.V...  1.28 us
  transfers between devices with their start and end apart: 2, of which 2 were waited for; matrix products, arithmetic and copies ran while one was open for 1% of the time, Pallas kernels for 0%

profile of v6, /device:TPU:6, one launch (start us, length us, event | category | flops | bytes accessed | tf_op | source)
XLA Modules:
  0.0 62.9 jit_solution(11243118988781939576)
XLA Ops:
  0.0 0.0 copy-start
  0.0 2.1 %project.1 = (bf16[8,64,512]{2,1,0:T(8,128)(2,1)S(1)}, bf16[4,128,512]{2,1,0:T(8,128)(2,1)S(1)}, bf16[16,512]{1,0:T(8,128)(2,1)S(1)}, bf16[16,512]{1,0:T(8,128)(2,1)S(1)}) custom-call(bf16[4,512,128]{2,1,0:T(8,128)(2,1)} %refs_0_.1, f32[1,128]{1,0:T(1,128)} %bitcast.28, f32[1,128]{1,0:T(1,128)} %bitcast.29, f32[1,64]{1,0:T(1,128)} %bitcast.30, ...), custom_call_target="tpu_custom_call" | custom-call | tf_op jit(solution)/shard_map/project/pallas_call | solution.py:87
  2.1 0.3 copy.16
  2.4 29.5 %all_to_all.10 = bf16[64,8,512]{2,1,0:T(8,128)(2,1)S(1)} all-to-all(bf16[64,8,512]{2,1,0:T(8,128)(2,1)S(1)} %copy.16), channel_id=1, replica_groups=mesh['x'=4,'z'=8,'ylo'=2,'core'=2,'yhi'=2] {'x','z','ylo'}, dimensions={0} | all-to-all | bytes 1048576 | tf_op jit(solution)/shard_map/all_to_all | solution.py:184
  31.9 0.1 slice.8
  32.0 0.1 collective-permute-start
  32.1 0.1 slice.7
  32.3 0.1 reshape.22
  32.3 1.3 %collective-permute-done = bf16[64,4,512]{2,1,0:T(4,128)(2,1)S(1)} collective-permute-done((bf16[64,4,512]{2,1,0:T(4,128)(2,1)S(1)}, bf16[64,4,512]{2,1,0:T(4,128)(2,1)S(1)}, u32[]{:S(2)}, u32[]{:S(2)}) %collective-permute-start) | collective-permute-done | bytes 262176 | tf_op jit(solution)/shard_map/ppermute | solution.py:186
  33.6 0.7 %convolution_convert_fusion = bf16[256,512]{1,0:T(8,128)(2,1)S(1)} fusion(bf16[256,512]{1,0:T(8,128)(2,1)S(1)} %reshape.22, bf16[64,4,512]{2,1,0:T(4,128)(2,1)S(1)} %collective-permute-done, bf16[64,4,512]{2,1,0:T(4,128)(2,1)S(1)} %slice.8, pred[]{:T(512)S(6)} %eq.3), kind=kOutput, calls=%fused_computation.5 | convolution fusion | flops 136708096 | bytes 1048577 | tf_op jit(solution)/shard_map/dot_general | solution.py:192
  34.3 0.1 reshape.23
  34.4 18.6 %all_to_all.11 = bf16[64,4,512]{2,1,0:T(4,128)(2,1)S(1)} all-to-all(bf16[64,4,512]{2,1,0:T(4,128)(2,1)S(1)} %reshape.23), channel_id=1, replica_groups=mesh['x'=4,'z'=8,'ylo'=2,'core'=2,'yhi'=2] {'x','z','ylo'}, dimensions={0} | all-to-all | bytes 524288 | tf_op jit(solution)/shard_map/all_to_all | solution.py:199
  53.1 3.0 %collective-permute-start.1 = (bf16[272,512]{1,0:T(8,128)(2,1)S(1)}, bf16[272,512]{1,0:T(8,128)(2,1)S(1)}, u32[]{:S(2)}, u32[]{:S(2)}) collective-permute-start(bf16[272,512]{1,0:T(8,128)(2,1)S(1)} %get-tuple-element.21), channel_id=1, source_target_pairs={{0,1},{1,0},{2,3},{3,2},{4,5},{5,4},{6,7},{7,6},{8,9},{9,8},{10,11... | collective-permute-start | bytes 835592 | tf_op jit(solution)/shard_map/ppermute | solution.py:201
  56.1 0.0 copy-done
  56.1 0.3 fusion.3.gate_ref
  56.4 5.3 %collective-permute-done.1.other_ref = bf16[272,512]{1,0:T(8,128)(2,1)S(1)} collective-permute-done((bf16[272,512]{1,0:T(8,128)(2,1)S(1)}, bf16[272,512]{1,0:T(8,128)(2,1)S(1)}, u32[]{:S(2)}, u32[]{:S(2)}) %collective-permute-start.1) | collective-permute-done | bytes 278560 | tf_op jit(solution)/shard_map/ppermute | solution.py:201
  61.6 1.3 %finish.1 = bf16[4,64,512]{2,1,0:T(8,128)(2,1)} custom-call(bf16[272,512]{1,0:T(8,128)(2,1)S(1)} %get-tuple-element.22.mine_ref, bf16[272,512]{1,0:T(8,128)(2,1)S(1)} %collective-permute-done.1.other_ref, f32[4,64,512]{2,1,0:T(8,128)S(1)} %fusion.3.gate_ref), custom_call_target="tpu_custom_call" | custom-call | tf_op jit(solution)/shard_map/finish/pallas_call | solution.py:148
  (2 shorter events, 0.1 us)
Async XLA Ops:
  0.0 56.1 %copy-start = (bf16[128,64]{0,1:T(8,128)(2,1)S(1)}, bf16[128,64]{0,1:T(8,128)(2,1)}, u32[]{:S(2)}) copy-start(bf16[128,64]{0,1:T(8,128)(2,1)} %param.21) | copy-start | bytes 49156
  32.0 1.6 %collective-permute-start = (bf16[64,4,512]{2,1,0:T(4,128)(2,1)S(1)}, bf16[64,4,512]{2,1,0:T(4,128)(2,1)S(1)}, u32[]{:S(2)}, u32[]{:S(2)}) collective-permute-start(bf16[64,4,512]{2,1,0:T(4,128)(2,1)S(1)} %slice.8), channel_id=1, source_target_pairs={{0,2},{2,0},{1,3},{3,1},{4,6},{6,4},{5,7},{7,5},{8,10},{10,8},{9,1... | collective-permute-start | bytes 786440 | tf_op jit(solution)/shard_map/ppermute | solution.py:186
  53.1 8.5 %collective-permute-start.1 = (bf16[272,512]{1,0:T(8,128)(2,1)S(1)}, bf16[272,512]{1,0:T(8,128)(2,1)S(1)}, u32[]{:S(2)}, u32[]{:S(2)}) collective-permute-start(bf16[272,512]{1,0:T(8,128)(2,1)S(1)} %get-tuple-element.21), channel_id=1, source_target_pairs={{0,1},{1,0},{2,3},{3,2},{4,5},{5,4},{6,7},{7,6},{8,9},{9,8},{10,11... | collective-permute-start | bytes 835592 | tf_op jit(solution)/shard_map/ppermute | solution.py:201

commit v7 on v6

--- a/solution.py
+++ b/solution.py
@@ -63,12 +63,13 @@
     normed = centred * lax.rsqrt(var + EPS) * scales[:, 0:1] + scales[:, 8:9]
     normed = normed.astype(BF16)
     pre = jnp.dot(weight_buf[...], normed, preferred_element_type=F32)
+    left, right = [], []
     for i in range(rows):
         at = slice(i * tokens, (i + 1) * tokens)
         normed_ref[i] = normed[:, at]
-        sent_ref[rows + i] = (sigmoid(pre[:own, at]) * pre[own : 2 * own, at]).astype(BF16)
-        right = sigmoid(pre[2 * own : 3 * own, at]) * pre[3 * own :, at]
-        sent_ref[i] = right.astype(BF16)
+        left.append((sigmoid(pre[:own, at]) * pre[own : 2 * own, at]).astype(BF16))
+        right.append((sigmoid(pre[2 * own : 3 * own, at]) * pre[3 * own :, at]).astype(BF16))
+    sent_ref[...] = jnp.swapaxes(jnp.stack(right + left, 0), 0, 1)
 
     pieces = [piece.astype(F32) for n in (0, 8) for piece in split3(tri_buf[n : n + 1])]
     pieces = jnp.concatenate(pieces + [jnp.zeros_like(pieces[0])] * 2, 0).T
@@ -89,7 +90,7 @@
         in_specs=[pl.BlockSpec(memory_space=pl.ANY)] * 10,
         out_specs=[pl.BlockSpec(memory_space=pltpu.VMEM)] * 4,
         out_shape=[
-            pltpu.VMEM((2 * rows, own, tokens), BF16),
+            pltpu.VMEM((own, 2 * rows, tokens), BF16),
             pltpu.VMEM((rows, channels, tokens), BF16),
             pltpu.VMEM((16, 512), BF16),
             pltpu.VMEM((16, 512), BF16),
@@ -177,18 +178,16 @@
         [left_gate.T, left_weight.T, right_gate.T, right_weight.T],
         out_weight,
     )
-    sent = sent.transpose(1, 0, 2)
     first = lax.axis_index("core") == 0
     sent, first = lax.optimization_barrier((sent, first))
 
     got = lax.all_to_all(sent, CHIPS, 0, 0, tiled=True)
     right_own, got = lax.optimization_barrier((got[:, :rows], got))
     right_other = lax.ppermute(right_own, "core", SWAP)
-    right_all = jnp.where(
-        first,
-        jnp.concatenate([right_own, right_other], 1),
-        jnp.concatenate([right_other, right_own], 1),
-    )
+    own_twice = jnp.concatenate([right_own, right_own], 1)
+    right_other, own_twice = lax.optimization_barrier((right_other, own_twice))
+    from_own = (lax.broadcasted_iota(jnp.int32, (1, 2 * rows, 1), 1) < rows) == first
+    right_all = jnp.where(from_own, own_twice, jnp.concatenate([right_other, right_other], 1))
     triangle = lax.dot_general(
         got[:, rows:].reshape(-1, tokens),
         right_all.reshape(-1, tokens),

time: 63.1 us -> 62.8 us (level)
  no operation moved by 1% of the time
where the time goes in v7:
time: 62.8 us; the launch traced here: 62.5 us
  blocking collectives  48.1 us (77%)
  waiting for transfers between devices  6.33 us (10%)
  Pallas kernels  3.45 us (5%)
  starting transfers between devices  3.07 us (5%)
  matrix products  0.82 us (1%)
    all_to_all x1, blocking collectives, body(): got = lax.all_to_all(sent, CHIPS, 0, 0, tiled=True)  29.5 us
    all_to_all x1, blocking collectives, body(): lax.all_to_all(triangle.reshape(own, rows, tokens), CHIPS, 0, 0, tiled=True)  18.6 us
    ppermute x1, waiting for transfers between devices, body(): other = lax.ppermute(jnp.concatenate([tri, extra], 0), 'yhi', SWAP)  5.28 us
    ppermute x1, starting transfers between devices, body(): other = lax.ppermute(jnp.concatenate([tri, extra], 0), 'yhi', SWAP)  2.98 us
    pallas_call x1, Pallas kernels, project(): pl.pallas_call(project_kernel, in_specs=[pl.BlockSpec(memory_space=pl.ANY...  2.17 us
    pallas_call x1, Pallas kernels, finish(): pl.pallas_call(finish_kernel, in_specs=[pl.BlockSpec(memory_space=pltpu.V...  1.28 us
  transfers between devices with their start and end apart: 2, of which 2 were waited for; matrix products, arithmetic and copies ran while one was open for 1% of the time, Pallas kernels for 0%

profile of v7, /device:TPU:6, one launch (start us, length us, event | category | flops | bytes accessed | tf_op | source)
XLA Modules:
  0.0 62.5 jit_solution(2789778034544945929)
XLA Ops:
  0.0 0.0 copy-start
  0.0 2.2 %project.1 = (bf16[64,8,512]{2,1,0:T(8,128)(2,1)S(1)}, bf16[4,128,512]{2,1,0:T(8,128)(2,1)S(1)}, bf16[16,512]{1,0:T(8,128)(2,1)S(1)}, bf16[16,512]{1,0:T(8,128)(2,1)S(1)}) custom-call(bf16[4,512,128]{2,1,0:T(8,128)(2,1)} %refs_0_.1, f32[1,128]{1,0:T(1,128)} %bitcast.26, f32[1,128]{1,0:T(1,128)} %bitcast.27, f32[1,64]{1,0:T(1,128)} %bitcast.28, ...), custom_call_target="tpu_custom_call" | custom-call | tf_op jit(solution)/shard_map/project/pallas_call | solution.py:88
  2.2 29.5 %all_to_all.10 = bf16[64,8,512]{2,1,0:T(8,128)(2,1)S(1)} all-to-all(bf16[64,8,512]{2,1,0:T(8,128)(2,1)S(1)} %get-tuple-element.16), channel_id=1, replica_groups=mesh['x'=4,'z'=8,'ylo'=2,'core'=2,'yhi'=2] {'x','z','ylo'}, dimensions={0} | all-to-all | bytes 1048576 | tf_op jit(solution)/shard_map/all_to_all | solution.py:184
  31.7 0.1 slice.8
  31.8 0.1 collective-permute-start
  31.9 0.1 slice.7
  32.1 0.1 reshape.19
  32.1 0.2 pad_maximum_fusion
  32.4 1.1 %collective-permute-done = bf16[64,4,512]{2,1,0:T(4,128)(2,1)S(1)} collective-permute-done((bf16[64,4,512]{2,1,0:T(4,128)(2,1)S(1)}, bf16[64,4,512]{2,1,0:T(4,128)(2,1)S(1)}, u32[]{:S(2)}, u32[]{:S(2)}) %collective-permute-start) | collective-permute-done | bytes 262176 | tf_op jit(solution)/shard_map/ppermute | solution.py:186
  33.4 0.5 convolution_convert_fusion
  34.0 0.1 reshape.21
  34.0 18.6 %all_to_all.11 = bf16[64,4,512]{2,1,0:T(4,128)(2,1)S(1)} all-to-all(bf16[64,4,512]{2,1,0:T(4,128)(2,1)S(1)} %reshape.21), channel_id=1, replica_groups=mesh['x'=4,'z'=8,'ylo'=2,'core'=2,'yhi'=2] {'x','z','ylo'}, dimensions={0} | all-to-all | bytes 524288 | tf_op jit(solution)/shard_map/all_to_all | solution.py:198
  52.7 3.0 %collective-permute-start.1 = (bf16[272,512]{1,0:T(8,128)(2,1)S(1)}, bf16[272,512]{1,0:T(8,128)(2,1)S(1)}, u32[]{:S(2)}, u32[]{:S(2)}) collective-permute-start(bf16[272,512]{1,0:T(8,128)(2,1)S(1)} %get-tuple-element.25), channel_id=1, source_target_pairs={{0,1},{1,0},{2,3},{3,2},{4,5},{5,4},{6,7},{7,6},{8,9},{9,8},{10,11... | collective-permute-start | bytes 835592 | tf_op jit(solution)/shard_map/ppermute | solution.py:200
  55.7 0.0 copy-done
  55.7 0.3 fusion.3.gate_ref
  56.0 5.3 %collective-permute-done.1.other_ref = bf16[272,512]{1,0:T(8,128)(2,1)S(1)} collective-permute-done((bf16[272,512]{1,0:T(8,128)(2,1)S(1)}, bf16[272,512]{1,0:T(8,128)(2,1)S(1)}, u32[]{:S(2)}, u32[]{:S(2)}) %collective-permute-start.1) | collective-permute-done | bytes 278560 | tf_op jit(solution)/shard_map/ppermute | solution.py:200
  61.3 1.3 %finish.1 = bf16[4,64,512]{2,1,0:T(8,128)(2,1)} custom-call(bf16[272,512]{1,0:T(8,128)(2,1)S(1)} %get-tuple-element.26.mine_ref, bf16[272,512]{1,0:T(8,128)(2,1)S(1)} %collective-permute-done.1.other_ref, f32[4,64,512]{2,1,0:T(8,128)S(1)} %fusion.3.gate_ref), custom_call_target="tpu_custom_call" | custom-call | tf_op jit(solution)/shard_map/finish/pallas_call | solution.py:149
  (3 shorter events, 0.1 us)
Async XLA Ops:
  0.0 55.7 %copy-start = (bf16[128,64]{0,1:T(8,128)(2,1)S(1)}, bf16[128,64]{0,1:T(8,128)(2,1)}, u32[]{:S(2)}) copy-start(bf16[128,64]{0,1:T(8,128)(2,1)} %param.21) | copy-start | bytes 49156
  31.8 1.6 %collective-permute-start = (bf16[64,4,512]{2,1,0:T(4,128)(2,1)S(1)}, bf16[64,4,512]{2,1,0:T(4,128)(2,1)S(1)}, u32[]{:S(2)}, u32[]{:S(2)}) collective-permute-start(bf16[64,4,512]{2,1,0:T(4,128)(2,1)S(1)} %slice.8), channel_id=1, source_target_pairs={{0,2},{2,0},{1,3},{3,1},{4,6},{6,4},{5,7},{7,5},{8,10},{10,8},{9,1... | collective-permute-start | bytes 786440 | tf_op jit(solution)/shard_map/ppermute | solution.py:186
  52.7 8.6 %collective-permute-start.1 = (bf16[272,512]{1,0:T(8,128)(2,1)S(1)}, bf16[272,512]{1,0:T(8,128)(2,1)S(1)}, u32[]{:S(2)}, u32[]{:S(2)}) collective-permute-start(bf16[272,512]{1,0:T(8,128)(2,1)S(1)} %get-tuple-element.25), channel_id=1, source_target_pairs={{0,1},{1,0},{2,3},{3,2},{4,5},{5,4},{6,7},{7,6},{8,9},{9,8},{10,11... | collective-permute-start | bytes 835592 | tf_op jit(solution)/shard_map/ppermute | solution.py:200

commit v8 on v7

--- a/solution.py
+++ b/solution.py
@@ -39,8 +39,8 @@
 
 def project_kernel(*refs):
     pair_ref, scale_refs, weight_refs, out_weight_ref = refs[0], refs[1:5], refs[5:9], refs[9]
-    sent_ref, normed_ref, extra_ref, extra_own_ref = refs[10:14]
-    pair_buf, scale_buf, tri_buf, weight_buf, out_weight_buf, sem, sems = refs[14:]
+    sent_ref, normed_ref, out_weight_buf, tri_buf = refs[10:14]
+    pair_buf, scale_buf, weight_buf, sem, sems = refs[14:]
     rows, tokens, channels = pair_buf.shape
     own = weight_refs[0].shape[0]
     load = pltpu.make_async_copy(pair_ref, pair_buf, sem)
@@ -53,12 +53,19 @@
         copies.append(pltpu.make_async_copy(weight_refs[n], place, sems.at[4 + n]))
     for copy in copies:
         copy.start()
+    row = lax.broadcasted_iota(jnp.int32, (channels, channels), 0)
+    column = lax.broadcasted_iota(jnp.int32, (channels, channels), 1)
+    centre = (jnp.where(row == column, 1.0, 0.0) - 1 / channels).astype(BF16)
     for copy in copies + [load]:
         copy.wait()
 
     scales = scale_buf[...].T
-    values = pair_buf[...].reshape(rows * tokens, channels).T.astype(F32)
-    centred = values - jnp.mean(values, 0, keepdims=True)
+    centred = lax.dot_general(
+        centre,
+        pair_buf[...].reshape(rows * tokens, channels),
+        (((1,), (1,)), ((), ())),
+        preferred_element_type=F32,
+    )
     var = jnp.mean(centred * centred, 0, keepdims=True)
     normed = centred * lax.rsqrt(var + EPS) * scales[:, 0:1] + scales[:, 8:9]
     normed = normed.astype(BF16)
@@ -71,15 +78,29 @@
         right.append((sigmoid(pre[2 * own : 3 * own, at]) * pre[3 * own :, at]).astype(BF16))
     sent_ref[...] = jnp.swapaxes(jnp.stack(right + left, 0), 0, 1)
 
-    pieces = [piece.astype(F32) for n in (0, 8) for piece in split3(tri_buf[n : n + 1])]
+
+def pack_kernel(out_weight_ref, tri_ref, extra_ref, extra_own_ref):
+    own, channels = out_weight_ref.shape
+    pieces = [piece.astype(F32) for n in (0, 8) for piece in split3(tri_ref[n : n + 1])]
     pieces = jnp.concatenate(pieces + [jnp.zeros_like(pieces[0])] * 2, 0).T
     blank = jnp.zeros((own, channels - own - 8), F32)
-    columns = out_weight_buf[...].astype(F32).T
+    columns = out_weight_ref[...].astype(F32).T
     low = lax.axis_index("yhi") == 0
     mine = jnp.where(low, columns[:own], columns[own:])
     theirs = jnp.where(low, columns[own:], columns[:own])
     extra_ref[...] = pack(jnp.concatenate([pieces, blank, theirs], 1))
     extra_own_ref[...] = pack(jnp.concatenate([mine, pieces, blank], 1))
+
+
+def pack_extra(out_weight, scales):
+    operands = [pltpu.with_memory_space_constraint(a, pltpu.VMEM) for a in (out_weight, scales)]
+    return pl.pallas_call(
+        pack_kernel,
+        in_specs=[pl.BlockSpec(memory_space=pltpu.VMEM)] * 2,
+        out_specs=[pl.BlockSpec(memory_space=pltpu.VMEM)] * 2,
+        out_shape=[pltpu.VMEM((16, 512), BF16)] * 2,
+        name="pack",
+    )(*operands)
 
 
 def project(pair, scales, weights, out_weight):
@@ -92,15 +113,13 @@
         out_shape=[
             pltpu.VMEM((own, 2 * rows, tokens), BF16),
             pltpu.VMEM((rows, channels, tokens), BF16),
-            pltpu.VMEM((16, 512), BF16),
-            pltpu.VMEM((16, 512), BF16),
+            pltpu.VMEM((own, channels), BF16),
+            pltpu.VMEM((16, own), F32),
         ],
         scratch_shapes=[
             pltpu.VMEM((rows, tokens, channels), BF16),
             pltpu.VMEM((16, channels), F32),
-            pltpu.VMEM((16, own), F32),
             pltpu.VMEM((4 * own, channels), BF16),
-            pltpu.VMEM((own, channels), BF16),
             pltpu.SemaphoreType.DMA,
             pltpu.SemaphoreType.DMA((9,)),
         ],
@@ -172,7 +191,7 @@
     rows, tokens, channels = pair.shape
     own = left_weight.shape[1]
 
-    sent, normed, extra, extra_own = project(
+    sent, normed, out_raw, tri_raw = project(
         pair,
         [norm_gain, norm_bias, tri_gain, tri_bias],
         [left_gate.T, left_weight.T, right_gate.T, right_weight.T],
@@ -182,10 +201,15 @@
     sent, first = lax.optimization_barrier((sent, first))
 
     got = lax.all_to_all(sent, CHIPS, 0, 0, tiled=True)
-    right_own, got = lax.optimization_barrier((got[:, :rows], got))
+    right_own, got, out_raw, tri_raw = lax.optimization_barrier(
+        (got[:, :rows], got, out_raw, tri_raw)
+    )
     right_other = lax.ppermute(right_own, "core", SWAP)
     own_twice = jnp.concatenate([right_own, right_own], 1)
-    right_other, own_twice = lax.optimization_barrier((right_other, own_twice))
+    extra, extra_own = pack_extra(out_raw, tri_raw)
+    right_other, own_twice, extra, extra_own = lax.optimization_barrier(
+        (right_other, own_twice, extra, extra_own)
+    )
     from_own = (lax.broadcasted_iota(jnp.int32, (1, 2 * rows, 1), 1) < rows) == first
     right_all = jnp.where(from_own, own_twice, jnp.concatenate([right_other, right_other], 1))
     triangle = lax.dot_general(

time: 62.8 us -> 62.7 us (level)
  no operation moved by 1% of the time
where the time goes in v8:
time: 62.7 us; the launch traced here: 62.4 us
  blocking collectives  48.1 us (77%)
  waiting for transfers between devices  6.14 us (10%)
  Pallas kernels  3.53 us (6%)
  starting transfers between devices  3.09 us (5%)
  matrix products  0.82 us (1%)
    all_to_all x1, blocking collectives, body(): got = lax.all_to_all(sent, CHIPS, 0, 0, tiled=True)  29.5 us
    all_to_all x1, blocking collectives, body(): lax.all_to_all(triangle.reshape(own, rows, tokens), CHIPS, 0, 0, tiled=True)  18.6 us
    ppermute x1, waiting for transfers between devices, body(): other = lax.ppermute(jnp.concatenate([tri, extra], 0), 'yhi', SWAP)  5.26 us
    ppermute x1, starting transfers between devices, body(): other = lax.ppermute(jnp.concatenate([tri, extra], 0), 'yhi', SWAP)  2.99 us
    pallas_call x1, Pallas kernels, project(): pl.pallas_call(project_kernel, in_specs=[pl.BlockSpec(memory_space=pl.ANY...  2.08 us
    pallas_call x1, Pallas kernels, finish(): pl.pallas_call(finish_kernel, in_specs=[pl.BlockSpec(memory_space=pltpu.V...  1.28 us
  transfers between devices with their start and end apart: 2, of which 2 were waited for; matrix products, arithmetic and copies ran while one was open for 1% of the time, Pallas kernels for 0%

profile of v8, /device:TPU:6, one launch (start us, length us, event | category | flops | bytes accessed | tf_op | source)
XLA Modules:
  0.0 62.4 jit_solution(7470199560170284354)
XLA Ops:
  0.0 0.0 copy-start
  0.0 2.1 %project.1 = (bf16[64,8,512]{2,1,0:T(8,128)(2,1)S(1)}, bf16[4,128,512]{2,1,0:T(8,128)(2,1)S(1)}, bf16[64,128]{1,0:T(8,128)(2,1)S(1)}, f32[16,64]{1,0:T(8,128)S(1)}) custom-call(bf16[4,512,128]{2,1,0:T(8,128)(2,1)} %refs_0_.1, f32[1,128]{1,0:T(1,128)} %bitcast.26, f32[1,128]{1,0:T(1,128)} %bitcast.27, f32[1,64]{1,0:T(1,128)} %bitcast.28, f32[1,64]{1,0:T(1,128)} %bitcast.29, ...), custom_call_target="tpu_custom_call" | custom-call | tf_op jit(solution)/shard_map/project/pallas_call | solution.py:109
  2.1 29.5 %all_to_all.10 = bf16[64,8,512]{2,1,0:T(8,128)(2,1)S(1)} all-to-all(bf16[64,8,512]{2,1,0:T(8,128)(2,1)S(1)} %get-tuple-element.22), channel_id=1, replica_groups=mesh['x'=4,'z'=8,'ylo'=2,'core'=2,'yhi'=2] {'x','z','ylo'}, dimensions={0} | all-to-all | bytes 1048576 | tf_op jit(solution)/shard_map/all_to_all | solution.py:203
  31.6 0.1 slice.8
  31.7 0.1 collective-permute-start
  31.8 0.1 slice.7
  32.0 0.1 reshape.19
  32.0 0.2 pack.1
  32.2 0.2 pad_maximum_fusion
  32.4 0.9 %collective-permute-done = bf16[64,4,512]{2,1,0:T(4,128)(2,1)S(1)} collective-permute-done((bf16[64,4,512]{2,1,0:T(4,128)(2,1)S(1)}, bf16[64,4,512]{2,1,0:T(4,128)(2,1)S(1)}, u32[]{:S(2)}, u32[]{:S(2)}) %collective-permute-start) | collective-permute-done | bytes 262176 | tf_op jit(solution)/shard_map/ppermute | solution.py:207
  33.3 0.5 convolution_convert_fusion
  33.8 0.1 reshape.21
  33.9 18.6 %all_to_all.11 = bf16[64,4,512]{2,1,0:T(4,128)(2,1)S(1)} all-to-all(bf16[64,4,512]{2,1,0:T(4,128)(2,1)S(1)} %reshape.21), channel_id=1, replica_groups=mesh['x'=4,'z'=8,'ylo'=2,'core'=2,'yhi'=2] {'x','z','ylo'}, dimensions={0} | all-to-all | bytes 524288 | tf_op jit(solution)/shard_map/all_to_all | solution.py:222
  52.6 3.0 %collective-permute-start.1 = (bf16[272,512]{1,0:T(8,128)(2,1)S(1)}, bf16[272,512]{1,0:T(8,128)(2,1)S(1)}, u32[]{:S(2)}, u32[]{:S(2)}) collective-permute-start(bf16[272,512]{1,0:T(8,128)(2,1)S(1)} %get-tuple-element.37), channel_id=1, source_target_pairs={{0,1},{1,0},{2,3},{3,2},{4,5},{5,4},{6,7},{7,6},{8,9},{9,8},{10,11... | collective-permute-start | bytes 835592 | tf_op jit(solution)/shard_map/ppermute | solution.py:224
  55.6 0.0 copy-done
  55.6 0.3 fusion.3.gate_ref
  55.9 5.3 %collective-permute-done.1.other_ref = bf16[272,512]{1,0:T(8,128)(2,1)S(1)} collective-permute-done((bf16[272,512]{1,0:T(8,128)(2,1)S(1)}, bf16[272,512]{1,0:T(8,128)(2,1)S(1)}, u32[]{:S(2)}, u32[]{:S(2)}) %collective-permute-start.1) | collective-permute-done | bytes 278560 | tf_op jit(solution)/shard_map/ppermute | solution.py:224
  61.1 1.3 %finish.1 = bf16[4,64,512]{2,1,0:T(8,128)(2,1)} custom-call(bf16[272,512]{1,0:T(8,128)(2,1)S(1)} %get-tuple-element.38.mine_ref, bf16[272,512]{1,0:T(8,128)(2,1)S(1)} %collective-permute-done.1.other_ref, f32[4,64,512]{2,1,0:T(8,128)S(1)} %fusion.3.gate_ref), custom_call_target="tpu_custom_call" | custom-call | tf_op jit(solution)/shard_map/finish/pallas_call | solution.py:168
  (3 shorter events, 0.1 us)
Async XLA Ops:
  0.0 55.6 %copy-start = (bf16[128,64]{0,1:T(8,128)(2,1)S(1)}, bf16[128,64]{0,1:T(8,128)(2,1)}, u32[]{:S(2)}) copy-start(bf16[128,64]{0,1:T(8,128)(2,1)} %param.21) | copy-start | bytes 49156
  31.7 1.6 %collective-permute-start = (bf16[64,4,512]{2,1,0:T(4,128)(2,1)S(1)}, bf16[64,4,512]{2,1,0:T(4,128)(2,1)S(1)}, u32[]{:S(2)}, u32[]{:S(2)}) collective-permute-start(bf16[64,4,512]{2,1,0:T(4,128)(2,1)S(1)} %slice.8), channel_id=1, source_target_pairs={{0,2},{2,0},{1,3},{3,1},{4,6},{6,4},{5,7},{7,5},{8,10},{10,8},{9,1... | collective-permute-start | bytes 786440 | tf_op jit(solution)/shard_map/ppermute | solution.py:207
  52.6 8.6 %collective-permute-start.1 = (bf16[272,512]{1,0:T(8,128)(2,1)S(1)}, bf16[272,512]{1,0:T(8,128)(2,1)S(1)}, u32[]{:S(2)}, u32[]{:S(2)}) collective-permute-start(bf16[272,512]{1,0:T(8,128)(2,1)S(1)} %get-tuple-element.37), channel_id=1, source_target_pairs={{0,1},{1,0},{2,3},{3,2},{4,5},{5,4},{6,7},{7,6},{8,9},{9,8},{10,11... | collective-permute-start | bytes 835592 | tf_op jit(solution)/shard_map/ppermute | solution.py:224

commit v9 on v8

--- a/solution.py
+++ b/solution.py
@@ -137,10 +137,10 @@
     return gain, pieces[:, 3:4] + pieces[:, 4:5] + pieces[:, 5:6]
 
 
-def finish_kernel(mine_ref, other_ref, gate_ref, out_ref, done, sems):
+def finish_kernel(mine_ref, extra_ref, other_ref, gate_ref, out_ref, done, sems):
     rows, own, _ = gate_ref.shape
     size = rows * own
-    columns, columns_other = unpack(mine_ref[size:]), unpack(other_ref[size:])
+    columns, columns_other = unpack(extra_ref[...]), unpack(other_ref[size:])
     lane = lax.broadcasted_iota(jnp.int32, columns.shape, 1)
     weight = jnp.where(lane < own, columns.astype(F32), columns_other.astype(F32)).astype(BF16)
     gain, bias = scales_of(columns[:, own : own + 8].astype(F32))
@@ -162,12 +162,12 @@
         copy.wait()
 
 
-def finish(mine, other, gate_value):
-    rows, own, tokens = gate_value.shape
-    operands = [pltpu.with_memory_space_constraint(a, pltpu.VMEM) for a in (mine, other, gate_value)]
+def finish(*operands):
+    rows, own, tokens = operands[-1].shape
+    operands = [pltpu.with_memory_space_constraint(a, pltpu.VMEM) for a in operands]
     return pl.pallas_call(
         finish_kernel,
-        in_specs=[pl.BlockSpec(memory_space=pltpu.VMEM)] * 3,
+        in_specs=[pl.BlockSpec(memory_space=pltpu.VMEM)] * 4,
         out_specs=pl.BlockSpec(memory_space=pl.ANY),
         out_shape=jax.ShapeDtypeStruct((rows, own, tokens), BF16),
         scratch_shapes=[pltpu.VMEM((rows, own, tokens), BF16), pltpu.SemaphoreType.DMA((rows,))],
@@ -221,9 +221,10 @@
 
     tri = lax.all_to_all(triangle.reshape(own, rows, tokens), CHIPS, 0, 0, tiled=True)
     tri = tri.transpose(1, 0, 2).reshape(-1, tokens)
-    other = lax.ppermute(jnp.concatenate([tri, extra], 0), "yhi", SWAP)
+    mine = jnp.concatenate([tri, extra], 0)
+    other = lax.ppermute(mine, "yhi", SWAP)
     gate_value = jax.nn.sigmoid(per_row(out_gate.T, normed))
-    updated = finish(jnp.concatenate([tri, extra_own], 0), other, gate_value)
+    updated = finish(mine, extra_own, other, gate_value)
     return updated.transpose(0, 2, 1)
 
 

time: 62.7 us -> 62.6 us (level)
  no operation moved by 1% of the time
where the time goes in v9:
time: 62.6 us; the launch traced here: 62.4 us
  blocking collectives  48.1 us (77%)
  waiting for transfers between devices  6.14 us (10%)
  Pallas kernels  3.53 us (6%)
  starting transfers between devices  3.09 us (5%)
  matrix products  0.82 us (1%)
    all_to_all x1, blocking collectives, body(): got = lax.all_to_all(sent, CHIPS, 0, 0, tiled=True)  29.5 us
    all_to_all x1, blocking collectives, body(): lax.all_to_all(triangle.reshape(own, rows, tokens), CHIPS, 0, 0, tiled=True)  18.6 us
    ppermute x1, waiting for transfers between devices, body(): other = lax.ppermute(mine, 'yhi', SWAP)  5.26 us
    ppermute x1, starting transfers between devices, body(): other = lax.ppermute(mine, 'yhi', SWAP)  2.99 us
    pallas_call x1, Pallas kernels, project(): pl.pallas_call(project_kernel, in_specs=[pl.BlockSpec(memory_space=pl.ANY...  2.08 us
    pallas_call x1, Pallas kernels, finish(): pl.pallas_call(finish_kernel, in_specs=[pl.BlockSpec(memory_space=pltpu.V...  1.28 us
  transfers between devices with their start and end apart: 2, of which 2 were waited for; matrix products, arithmetic and copies ran while one was open for 1% of the time, Pallas kernels for 0%

profile of v9, /device:TPU:6, one launch (start us, length us, event | category | flops | bytes accessed | tf_op | source)
XLA Modules:
  0.0 62.4 jit_solution(2054764571169741831)
XLA Ops:
  0.0 0.0 copy-start
  0.0 2.1 %project.1 = (bf16[64,8,512]{2,1,0:T(8,128)(2,1)S(1)}, bf16[4,128,512]{2,1,0:T(8,128)(2,1)S(1)}, bf16[64,128]{1,0:T(8,128)(2,1)S(1)}, f32[16,64]{1,0:T(8,128)S(1)}) custom-call(bf16[4,512,128]{2,1,0:T(8,128)(2,1)} %refs_0_.1, f32[1,128]{1,0:T(1,128)} %bitcast.26, f32[1,128]{1,0:T(1,128)} %bitcast.27, f32[1,64]{1,0:T(1,128)} %bitcast.28, f32[1,64]{1,0:T(1,128)} %bitcast.29, ...), custom_call_target="tpu_custom_call" | custom-call | tf_op jit(solution)/shard_map/project/pallas_call | solution.py:109
  2.1 29.5 %all_to_all.10 = bf16[64,8,512]{2,1,0:T(8,128)(2,1)S(1)} all-to-all(bf16[64,8,512]{2,1,0:T(8,128)(2,1)S(1)} %get-tuple-element.22), channel_id=1, replica_groups=mesh['x'=4,'z'=8,'ylo'=2,'core'=2,'yhi'=2] {'x','z','ylo'}, dimensions={0} | all-to-all | bytes 1048576 | tf_op jit(solution)/shard_map/all_to_all | solution.py:203
  31.6 0.1 slice.8
  31.7 0.1 collective-permute-start
  31.8 0.1 slice.7
  32.0 0.1 reshape.19
  32.0 0.2 pack.1
  32.2 0.2 pad_maximum_fusion
  32.4 0.9 %collective-permute-done = bf16[64,4,512]{2,1,0:T(4,128)(2,1)S(1)} collective-permute-done((bf16[64,4,512]{2,1,0:T(4,128)(2,1)S(1)}, bf16[64,4,512]{2,1,0:T(4,128)(2,1)S(1)}, u32[]{:S(2)}, u32[]{:S(2)}) %collective-permute-start) | collective-permute-done | bytes 262176 | tf_op jit(solution)/shard_map/ppermute | solution.py:207
  33.3 0.5 convolution_convert_fusion
  33.8 0.1 reshape.21
  33.9 18.6 %all_to_all.11 = bf16[64,4,512]{2,1,0:T(4,128)(2,1)S(1)} all-to-all(bf16[64,4,512]{2,1,0:T(4,128)(2,1)S(1)} %reshape.21), channel_id=1, replica_groups=mesh['x'=4,'z'=8,'ylo'=2,'core'=2,'yhi'=2] {'x','z','ylo'}, dimensions={0} | all-to-all | bytes 524288 | tf_op jit(solution)/shard_map/all_to_all | solution.py:222
  52.6 3.0 %collective-permute-start.1 = (bf16[272,512]{1,0:T(8,128)(2,1)S(1)}, bf16[272,512]{1,0:T(8,128)(2,1)S(1)}, u32[]{:S(2)}, u32[]{:S(2)}) collective-permute-start(bf16[272,512]{1,0:T(8,128)(2,1)S(1)} %pad_maximum_fusion.1.mine_ref), channel_id=1, source_target_pairs={{0,1},{1,0},{2,3},{3,2},{4,5},{5,4},{6,7},{7,6},{8,9},{9,8},{10,11... | collective-permute-start | bytes 835592 | tf_op jit(solution)/shard_map/ppermute | solution.py:225
  55.6 0.0 copy-done
  55.6 0.3 fusion.3.gate_ref
  55.9 5.3 %collective-permute-done.1.other_ref = bf16[272,512]{1,0:T(8,128)(2,1)S(1)} collective-permute-done((bf16[272,512]{1,0:T(8,128)(2,1)S(1)}, bf16[272,512]{1,0:T(8,128)(2,1)S(1)}, u32[]{:S(2)}, u32[]{:S(2)}) %collective-permute-start.1) | collective-permute-done | bytes 278560 | tf_op jit(solution)/shard_map/ppermute | solution.py:225
  61.1 1.3 %finish.1 = bf16[4,64,512]{2,1,0:T(8,128)(2,1)} custom-call(bf16[272,512]{1,0:T(8,128)(2,1)S(1)} %pad_maximum_fusion.1.mine_ref, bf16[16,512]{1,0:T(8,128)(2,1)S(1)} %get-tuple-element.35.extra_ref, bf16[272,512]{1,0:T(8,128)(2,1)S(1)} %collective-permute-done.1.other_ref, f32[4,64,512]{2,1,0:T(8,128)S(1)} %fusion.3.gate_ref), custom_call_target="tpu_custom_call" | custom-call | tf_op jit(solution)/shard_map/finish/pallas_call | solution.py:168
  (3 shorter events, 0.1 us)
Async XLA Ops:
  0.0 55.6 %copy-start = (bf16[128,64]{0,1:T(8,128)(2,1)S(1)}, bf16[128,64]{0,1:T(8,128)(2,1)}, u32[]{:S(2)}) copy-start(bf16[128,64]{0,1:T(8,128)(2,1)} %param.21) | copy-start | bytes 49156
  31.7 1.6 %collective-permute-start = (bf16[64,4,512]{2,1,0:T(4,128)(2,1)S(1)}, bf16[64,4,512]{2,1,0:T(4,128)(2,1)S(1)}, u32[]{:S(2)}, u32[]{:S(2)}) collective-permute-start(bf16[64,4,512]{2,1,0:T(4,128)(2,1)S(1)} %slice.8), channel_id=1, source_target_pairs={{0,2},{2,0},{1,3},{3,1},{4,6},{6,4},{5,7},{7,5},{8,10},{10,8},{9,1... | collective-permute-start | bytes 786440 | tf_op jit(solution)/shard_map/ppermute | solution.py:207
  52.6 8.6 %collective-permute-start.1 = (bf16[272,512]{1,0:T(8,128)(2,1)S(1)}, bf16[272,512]{1,0:T(8,128)(2,1)S(1)}, u32[]{:S(2)}, u32[]{:S(2)}) collective-permute-start(bf16[272,512]{1,0:T(8,128)(2,1)S(1)} %pad_maximum_fusion.1.mine_ref), channel_id=1, source_target_pairs={{0,1},{1,0},{2,3},{3,2},{4,5},{5,4},{6,7},{7,6},{8,9},{9,8},{10,11... | collective-permute-start | bytes 835592 | tf_op jit(solution)/shard_map/ppermute | solution.py:225
